TPU v7x, 256 devices: a whole 4x4x8 slice. The times are simulated.
256 devices in a mesh: group: 32 (over y, z), head: 8 (over x, core).
Axes of the slice: x: 4, y: 4, z: 8, core: 2. Of those that a mesh axis runs over, the one named last changes fastest.
Arguments:
- query_states: bfloat16 [8192, 5120], P('group', 'head'), may hold values from -110 to 110
- key_states: bfloat16 [8192, 5120], P('group', 'head'), may hold values from -5 to 5
- value_states: bfloat16 [8192, 5120], P('group', 'head'), may hold values from -6 to 6
- hidden: bfloat16 [8192, 5120], P('group', 'head'), may hold values from -3 to 3
- out_weight: bfloat16 [5120, 5120], P('head'), may hold values from -0.078125 to 0.078125
- gate_table: float32 [1000, 5120], P(None, 'head'), may hold values from 0.3 to 3
- levels: int32 [64], P('group'), may hold values from 0 to 999
- visible: int32 [64, 64], replicated, may hold values 0 or 1
- incoming: bfloat16 [128, 5120], P(None, 'head'), may hold values from -6 to 6
Outputs:
- queue_next: bfloat16 [8192, 5120], P('group', 'head')
All inputs are finite; a program needn't handle non-finite values.
Results may differ from a plain program's by a relative error of at most 0.015.
Values may be sent and summed in bfloat16 or wider, within the bound.
A program may use at most 128 MiB of HBM per device.

v0:
```python
import jax
import jax.numpy as jnp
from jax import lax
from jax.sharding import PartitionSpec as P

HD = 128
TOK = 128


def from_behind(shard, axis, by):
    length = lax.axis_size(axis)
    pairs = [(i, i + by) for i in range(length) if 0 <= i + by < length]
    return lax.ppermute(shard, axis, pairs)


def block_attend(state, query, query_group, vis_rows, key_block, value_block, key_start):
    rows_block = key_block.shape[0]
    heads_dev = query.shape[1]
    first_group = key_start // TOK
    group_count = rows_block // TOK
    window = lax.dynamic_slice_in_dim(vis_rows, first_group, group_count, 1)
    group_ids = first_group + jnp.arange(group_count, dtype=jnp.int32)
    allowed_group = (group_ids[None, :] == query_group[:, None]) | (
        group_ids[None, :] < query_group[:, None]
    ) & (window == 1)
    scale = 1.0 / HD**0.5

    def compute(carry):
        row_max, row_total, weighted = carry
        allow = jnp.repeat(allowed_group, TOK, axis=1)
        key_heads = key_block.reshape(rows_block, heads_dev, HD)
        value_heads = value_block.reshape(rows_block, heads_dev, HD)
        scores = (
            jnp.einsum("qhd,khd->hqk", query, key_heads, preferred_element_type=jnp.float32) * scale
        )
        scores = jnp.where(allow[None], scores, -jnp.inf)
        new_max = jnp.maximum(row_max, jnp.max(scores, axis=2))
        safe_max = jnp.where(new_max == -jnp.inf, 0.0, new_max)
        keep_old = jnp.exp(row_max - safe_max)
        probs = jnp.exp(scores - safe_max[..., None])
        row_total = row_total * keep_old + jnp.sum(probs, axis=2)
        weighted = weighted * keep_old[..., None] + jnp.einsum(
            "hqk,khd->hqd",
            probs.astype(jnp.bfloat16),
            value_heads,
            preferred_element_type=jnp.float32,
        )
        return (new_max, row_total, weighted)

    def unchanged(carry):
        return carry

    return lax.cond(jnp.any(allowed_group), compute, unchanged, state)


def fold_rows(state, query, query_group, vis_rows, shard_rows, key_piece, value_piece):
    total_rows = key_piece.shape[0]
    step_rows = shard_rows * max(1, 512 // shard_rows)
    block_count = total_rows // step_rows

    def one_block(number, carry):
        offset = number * step_rows
        key_block = lax.dynamic_slice_in_dim(key_piece, offset, step_rows, 0)
        value_block = lax.dynamic_slice_in_dim(value_piece, offset, step_rows, 0)
        return block_attend(carry, query, query_group, vis_rows, key_block, value_block, offset)

    return lax.fori_loop(0, block_count, one_block, state)


def on_device(
    query_states,
    key_states,
    value_states,
    hidden,
    out_weight,
    gate_table,
    levels,
    visible,
    incoming,
):
    shard_rows = query_states.shape[0]
    width_dev = query_states.shape[1]
    heads_dev = width_dev // HD
    group_count = lax.axis_size("group")
    position = lax.axis_index("group")
    local_groups = shard_rows // TOK
    query_blocks = query_states.reshape(local_groups, TOK, width_dev)
    group_ids = position * local_groups + jnp.arange(local_groups, dtype=jnp.int32)
    query = query_blocks.reshape(shard_rows, heads_dev, HD)
    query_group = jnp.repeat(group_ids, TOK)
    vis_rows = jnp.repeat(jnp.take(visible, group_ids, axis=0), TOK, axis=0)
    start_state = (
        jnp.full((heads_dev, shard_rows), -jnp.inf, jnp.float32),
        jnp.zeros((heads_dev, shard_rows), jnp.float32),
        jnp.zeros((heads_dev, shard_rows, HD), jnp.float32),
    )
    state = fold_rows(
        start_state,
        query,
        query_group,
        vis_rows,
        shard_rows,
        lax.all_gather(key_states, "group", axis=0, tiled=True),
        lax.all_gather(value_states, "group", axis=0, tiled=True),
    )
    row_max, row_total, weighted = state
    mixed = weighted / row_total[..., None]
    attended = (
        jnp.transpose(mixed, (1, 0, 2)).reshape(local_groups, TOK, width_dev).astype(jnp.bfloat16)
    )
    attended = attended.reshape(shard_rows, width_dev)
    projected = jnp.dot(attended, out_weight, preferred_element_type=jnp.float32)
    summed = lax.psum_scatter(
        projected.astype(jnp.bfloat16), "head", scatter_dimension=1, tiled=True
    ).astype(jnp.float32)
    level_count = gate_table.shape[0]
    one_hot = (levels[:, None] == jnp.arange(level_count, dtype=jnp.int32)[None, :]).astype(
        jnp.float32
    )
    gate_rows = jnp.dot(one_hot, gate_table, precision=lax.Precision.HIGHEST)
    gates = jnp.repeat(gate_rows, TOK, axis=0)
    updated = (hidden.astype(jnp.float32) + gates * summed).astype(jnp.bfloat16)
    leading = updated[:TOK]
    arrived = from_behind(leading, "group", -1)
    arrived = jnp.where(position == group_count - 1, incoming, arrived)
    return jnp.concatenate([updated[TOK:], arrived], axis=0)


def solution(mesh):
    return jax.shard_map(
        on_device,
        mesh=mesh,
        in_specs=(
            P("group", "head"),
            P("group", "head"),
            P("group", "head"),
            P("group", "head"),
            P("head", None),
            P(None, "head"),
            P("group"),
            P(),
            P(None, "head"),
        ),
        out_specs=P("group", "head"),
        check_vma=False,
    )
```

profile of v0, /device:TPU:1, one launch (start us, length us, event | category | flops | bytes accessed | tf_op | source)
XLA Modules:
  0.0 416.2 jit_solution(14944639159334186659)
XLA Ops:
  6.5 2.0 copy.25
  8.6 1.9 copy.27
  10.6 1.3 gather_fusion
  11.9 0.1 broadcast_select_fusion.1
  12.0 0.1 copy.24
  12.1 0.1 broadcast_in_dim.76
  12.3 1.1 copy.26
  13.4 0.2 copy.28
  13.6 112.9 %all-gather.3.cloned.1.call-done = bf16[8192,640]{0,1:T(8,128)(2,1)} async-done(((bf16[256,640]{0,1:T(8,128)(2,1)}), bf16[8192,640]{0,1:T(8,128)(2,1)}) %all-gather.3.cloned.1.call-update) | async-done | bytes 10485776 | tf_op jit(solution)/shard_map/all_gather | solution.py:103
  126.5 114.6 %all-gather.5.cloned.1.call-done = bf16[8192,640]{0,1:T(8,128)(2,1)} async-done(((bf16[256,640]{0,1:T(8,128)(2,1)}), bf16[8192,640]{0,1:T(8,128)(2,1)}) %all-gather.5.cloned.1.call-update) | async-done | bytes 10485776 | tf_op jit(solution)/shard_map/all_gather | solution.py:104
  241.1 0.9 broadcast_in_dim.72
  242.0 30.2 %while.20 = (s32[]{:T(128)}, f32[5,256]{1,0:T(8,128)S(1)}, f32[5,256]{1,0:T(8,128)S(1)}, f32[5,256,128]{2,1,0:T(8,128)}, s32[256,64]{0,1:T(8,128)S(1)}, /*index=...) while((s32[]{:T(128)}, f32[5,256]{1,0:T(8,128)S(1)}, ...), condition=%wide.region_6.7_spmd.clone, body=%wide.region_0.6_spmd.clone.sunk | while | flops 343094816 | bytes 14054964 | solution.py:67
  242.1 0.8 fusion.35
  243.5 5.6 %conditional.3 = ((f32[5,256]{1,0:T(8,128)S(1)}, f32[5,256]{1,0:T(8,128)S(1)}, f32[5,256,128]{2,1,0:T(8,128)})) conditional(s32[]{:T(128)} %convert_element_type.57, (f32[5,256]{1,0:T(8,128)S(1)}, f32[5,256]{1,0:T(8,128)S(1)}, f32[5,256,128]{2,1,0:T(8,128)}) %tuple.69, (pred[256,4]{0,1:T(4,128)(4,1)S(1)}, s32[]{:T(128)}, pred[]{:T(512)}, ...), branch_computations={%region_2.2_spmd, %region_3.5_spmd} | conditional | flops 343088640 | bytes 14047293 | solution.py:53
  243.5 1.4 constant_dynamic-slice_fusion
  244.9 0.7 fusion.4
  245.6 0.6 fusion.3
  246.2 2.9 fusion.11
  249.2 0.8 fusion.35
  250.6 0.1 broadcast_bitcast_fusion.2
  250.7 0.8 fusion.35
  252.2 0.1 broadcast_bitcast_fusion.2
  252.3 0.8 fusion.35
  253.7 0.1 broadcast_bitcast_fusion.2
  253.8 0.8 fusion.35
  255.3 0.1 broadcast_bitcast_fusion.2
  255.3 0.8 fusion.35
  256.9 0.8 fusion.35
  258.4 0.8 fusion.35
  260.0 0.8 fusion.35
  261.5 0.8 fusion.35
  263.0 0.8 fusion.35
  264.6 0.8 fusion.35
  266.1 0.8 fusion.35
  267.7 0.8 fusion.35
  269.2 0.8 fusion.35
  270.8 0.8 fusion.35
  272.2 1.3 copy.29
  273.6 6.6 %convolution_convert_fusion = bf16[256,5120]{1,0:T(8,128)(2,1)} fusion(bf16[256,640]{0,1:T(8,128)(2,1)S(1)} %bitcast.50, bf16[640,5120]{1,0:T(8,128)(2,1)} %param.17), kind=kOutput, calls=%fused_computation.25 | convolution fusion | flops 1679032320 | bytes 9502720 | tf_op jit(solution)/shard_map/dot_general | solution.py:112
  280.2 4.4 %copy.33 = bf16[256,5120]{0,1:T(8,128)(2,1)} copy(bf16[256,5120]{1,0:T(8,128)(2,1)} %convolution_convert_fusion) | data formatting | bytes 5242880
  284.6 0.6 copy-done.2
  285.2 0.9 fusion.20
  286.2 115.3 %reduce-scatter.4.cloned.1.call-done = bf16[640,256]{1,0:T(8,128)(2,1)} async-done(((bf16[5120,256]{1,0:T(8,128)(2,1)}), bf16[640,256]{1,0:T(8,128)(2,1)}) %reduce-scatter.4.cloned.1.call-update) | async-done | bytes 327696
  401.5 1.2 copy.34
  402.7 0.1 fusion.19
  402.8 1.3 collective-permute-start
  404.1 4.8 %collective-permute-done = bf16[128,640]{1,0:T(8,128)(2,1)S(1)} collective-permute-done((bf16[128,640]{1,0:T(8,128)(2,1)S(1)}, bf16[128,640]{1,0:T(8,128)(2,1)S(1)}, u32[]{:S(2)}, u32[]{:S(2)}) %collective-permute-start) | collective-permute-done | bytes 163872 | tf_op jit(solution)/shard_map/ppermute | solution.py:13
  408.9 0.8 pad_maximum_fusion
  (68 shorter events, 1.5 us)
Async XLA Ops:
  6.5 278.1 %copy-start = (f32[1000,640]{1,0:T(8,128)S(1)}, f32[1000,640]{1,0:T(8,128)}, u32[]{:S(2)}) copy-start(f32[1000,640]{1,0:T(8,128)} %param.18) | copy-start | bytes 7680004
  6.5 120.0 %all-gather.3.cloned.1.call-start = ((), (), s32[]{:S(2)}) async-start(), calls=%async_computation.1 | async-start | bytes 10813440 | tf_op jit(solution)/shard_map/all_gather | solution.py:103
  8.6 232.5 %all-gather.5.cloned.1.call-start = ((), (), s32[]{:S(2)}) async-start(), calls=%async_computation.2 | async-start | bytes 10813440 | tf_op jit(solution)/shard_map/all_gather | solution.py:104
  10.5 391.0 %reduce-scatter.4.cloned.1.call-start = ((), (), s32[]{:S(2)}) async-start(), calls=%async_computation.3 | async-start | bytes 2949120
  284.6 0.7 copy-start.2
  284.6 118.1 %copy-start.1 = (bf16[256,640]{1,0:T(8,128)(2,1)S(1)}, bf16[256,640]{1,0:T(8,128)(2,1)}, u32[]{:S(2)}) copy-start(bf16[256,640]{1,0:T(8,128)(2,1)} %param.16) | copy-start | bytes 983044
  402.8 6.1 %collective-permute-start = (bf16[128,640]{1,0:T(8,128)(2,1)S(1)}, bf16[128,640]{1,0:T(8,128)(2,1)S(1)}, u32[]{:S(2)}, u32[]{:S(2)}) collective-permute-start(bf16[128,640]{1,0:T(8,128)(2,1)S(1)} %get-tuple-element.416), channel_id=1, source_target_pairs={{8,0},{16,8},{24,16},{32,24},{40,32},{48,40},{56,48},{64,56},{72,6... | collective-permute-start | bytes 491528 | tf_op jit(solution)/shard_map/ppermute | solution.py:13
Sparse Core Ops, SparseCore 0:
  9.8 116.6 all-gather.2
  129.0 112.0 all-gather.4
  284.7 116.7 reduce-scatter.3
where the time goes:
time: 422 us; the launch traced here: 416 us
  waiting for transfers between devices  348 us (82%)
  local copies, waits for them, and re-layouts  17.7 us (4%)
  other arithmetic  14 us (3%)
  between operations  13.2 us (3%)
  loops' own time  11.1 us (3%)
  matrix products  11.1 us (3%)
    unnamed x4, waiting for transfers between devices  115 us
    all_gather x1, waiting for transfers between devices, on_device(): lax.all_gather(value_states, 'group', axis=0, tiled=True)  115 us
    all_gather x1, waiting for transfers between devices, on_device(): lax.all_gather(key_states, 'group', axis=0, tiled=True)  113 us
    reduce_or x16, other arithmetic, block_attend(): return lax.cond(jnp.any(allowed_group), compute, unchanged, state)  12.3 us
    unnamed x13, local copies, waits for them, and re-layouts  11.4 us
    another operation x1, loops' own time, fold_rows(): return lax.fori_loop(0, block_count, one_block, state)  10.8 us
  transfers between devices with their start and end apart: 4, of which 4 were waited for; matrix products, arithmetic and copies ran while one was open for 1% of the time, Pallas kernels for 0%

commit v1 on v0

v1 whole, which is shorter than its diff:
```python
import functools
import math

import jax
import jax.numpy as jnp
from jax import lax
from jax.experimental import pallas as pl
from jax.experimental.pallas import tpu as pltpu
from jax.sharding import PartitionSpec as P

HD = 128
TOK = 128
NY, NZ = 4, 8
NX = 4
PAIRS = NY * NZ
LOCAL_HEADS = 5
MAIN_TEAM, EXTRA_TEAM = 6, 8
SLOTS = 6
BIG = 1e30
MESH = pl.DeviceIdType.MESH
VMEM = pl.BlockSpec(memory_space=pltpu.VMEM)
ANY = pl.BlockSpec(memory_space=pl.ANY)


def coords():
    p = lax.axis_index("group")
    hd = lax.axis_index("head")
    return p // NZ, p % NZ, hd // 2, hd % 2


def remote(src, dst, send, recv, p, hd):
    return pltpu.make_async_remote_copy(
        src_ref=src,
        dst_ref=dst,
        send_sem=send,
        recv_sem=recv,
        device_id=(p, hd),
        device_id_type=MESH,
    )


def team():
    y, z, x, c = coords()
    col = z % 4
    half = z // 4
    extra = y == col
    size = jnp.where(extra, EXTRA_TEAM, MAIN_TEAM)
    rank = jnp.where(extra, 2 * col + c, 2 * ((y - col - 1 + NY) % NY) + c)
    head = jnp.where(extra, 4, col)
    return extra, size, rank, half, head


def pair_of(slot, size, rank):
    pos = jnp.where(slot % 2 == 0, rank, size - 1 - rank)
    return PAIRS - 1 - (slot * size + pos)


def owner_of(pair, head, x, c):
    size = MAIN_TEAM if head < 4 else EXTRA_TEAM
    t = PAIRS - 1 - pair
    slot = t // size
    pos = t % size
    rank = jnp.where(slot % 2 == 0, pos, size - 1 - pos)
    chip = rank // 2
    if head < 4:
        yd, zd = (head + 1 + chip) % NY, 4 * c + head
    else:
        yd, zd = chip, 4 * c + chip
    return yd * NZ + zd, 2 * x + rank % 2, slot


def gather_kernel(
    q_ref, k_ref, v_ref, buf, qbuf, qt, vt, qsend, ksend, vsend, qrecv, rmain, rextra, rsib, snext, sprev, enext, eprev, ssib
):
    y, z, x, c = coords()
    p = y * NZ + z
    hd = 2 * x + c
    extra, size, rank, half, head_in = team()
    col = z % 4

    def put(src, dst, send, recv, pd, hdd):
        me = jnp.logical_and(pd == p, hdd == hd)

        @pl.when(me)
        def _():
            pltpu.make_async_copy(src, dst, recv).start()

        @pl.when(jnp.logical_not(me))
        def _():
            remote(src, dst, send, recv, pd, hdd).start()

    def put_done(src, dst, send, recv, pd, hdd):
        me = jnp.logical_and(pd == p, hdd == hd)

        @pl.when(jnp.logical_not(me))
        def _():
            remote(src, dst, send, recv, pd, hdd).wait_send()

    def k_args(h):
        zd = 4 * c + h if h < 4 else 4 * c + y
        idx = jnp.where(y == h, 2, 0) if h < 4 else 0
        sems = rmain if h < 4 else rextra
        return (k_ref.at[:, pl.ds(h * HD, HD)], buf.at[idx, p], ksend.at[h], sems.at[p], y * NZ + zd, 2 * x)

    def v_args(h):
        zd = 4 * c + h if h < 4 else 4 * c + y
        idx = jnp.where(y == h, 2, 1) if h < 4 else 1
        sems = rmain if h < 4 else rextra
        return (vt.at[h], buf.at[idx, p], vsend.at[h], sems.at[p], y * NZ + zd, 2 * x + 1)

    def q_args(h):
        pd, hdd, slot = owner_of(p, h, x, c)
        return (qt.at[h], qbuf.at[slot], qsend.at[h], qrecv.at[slot], pd, hdd)

    for h in range(LOCAL_HEADS):
        put(*k_args(h))
    for h in range(LOCAL_HEADS):
        for g in range(2):
            vt[h, g * TOK : (g + 1) * TOK, :] = v_ref[g * TOK : (g + 1) * TOK, h * HD : (h + 1) * HD].T
        put(*v_args(h))
    for h in range(LOCAL_HEADS):
        qt[h] = q_ref[:, h * HD : (h + 1) * HD].T
        put(*q_args(h))

    yn, yp, yo = (y + 1) % NY, (y + 3) % NY, (y + 2) % NY

    def ring(step, main):
        if main:
            mine = jnp.where(extra, 2, c)
            there = lambda yd: jnp.where(yd == col, 2, c)
            zn, zp = z, z
            sems, to_next, to_prev = rmain, snext, sprev
        else:
            mine = c
            there = lambda yd: c
            zn, zp = 4 * half + yn, 4 * half + yp
            sems, to_next, to_prev = rextra, enext, eprev
        pn, pp = yn * NZ + zn, yp * NZ + zp

        def arrive(i):
            remote(buf.at[mine, i], buf.at[mine, i], to_next.at[0], sems.at[i], pn, hd).wait_recv()

        def go_next(i, s):
            return remote(buf.at[mine, i], buf.at[there(yn), i], to_next.at[s], sems.at[i], pn, hd)

        def go_prev(i, s):
            return remote(buf.at[mine, i], buf.at[there(yp), i], to_prev.at[s], sems.at[i], pp, hd)

        def sibling(i):
            copy = remote(buf.at[c, i], buf.at[c, i], ssib.at[i], rsib.at[i], p, 2 * x + 1 - c)
            if main:

                @pl.when(jnp.logical_not(extra))
                def _():
                    copy.start()
            else:
                copy.start()

        def own(b, carry):
            i = y * NZ + b
            arrive(i)
            go_next(i, b).start()
            go_prev(i, b).start()
            sibling(i)
            return carry

        def forward(b, carry):
            i = yp * NZ + b
            arrive(i)
            go_next(i, 8 + b).start()
            sibling(i)
            i = yn * NZ + 4 + b
            arrive(i)
            go_prev(i, 8 + b).start()
            sibling(i)
            return carry

        def rest(b, carry):
            for i in (yp * NZ + 4 + b, yn * NZ + b, yo * NZ + b, yo * NZ + 4 + b):
                arrive(i)
                sibling(i)
            return carry

        def close(b, carry):
            go_next(b, b).wait_send()
            go_prev(b, b).wait_send()
            return carry

        if step == 0:
            lax.fori_loop(0, NZ, own, 0)
        elif step == 1:
            lax.fori_loop(0, 4, forward, 0)
        elif step == 2:
            lax.fori_loop(0, 4, rest, 0)
        else:
            lax.fori_loop(0, 12, close, 0)

    for step in range(4):
        ring(step, True)

        @pl.when(extra)
        def _():
            ring(step, False)

    def sib_done(i, carry):
        remote(buf.at[c, i], buf.at[c, i], ssib.at[i], rsib.at[i], p, 2 * x + 1 - c).wait_send()
        remote(buf.at[1 - c, i], buf.at[1 - c, i], ssib.at[i], rsib.at[i], p, 2 * x + 1 - c).wait_recv()
        return carry

    lax.fori_loop(0, PAIRS, sib_done, 0)
    for h in range(LOCAL_HEADS):
        put_done(*k_args(h))
        put_done(*v_args(h))
        put_done(*q_args(h))
    for slot in range(SLOTS):

        @pl.when(pair_of(slot, size, rank) >= 0)
        def _():
            remote(qt.at[0], qbuf.at[slot], qsend.at[0], qrecv.at[slot], p, hd).wait_recv()


def attend_kernel(kv_ref, q_ref, vis_ref, o_ref, bias):
    extra, size, rank, half, head = team()
    scale = math.log2(math.e) / math.sqrt(HD)
    seen = (vis_ref[...] == 1).astype(jnp.float32).astype(jnp.bfloat16)

    def one_slot(slot, carry):
        pair = pair_of(slot, size, rank)
        group = 2 * pair + (lax.broadcasted_iota(jnp.int32, (64, 2 * TOK), 1) >= TOK).astype(jnp.int32)
        row = lax.broadcasted_iota(jnp.int32, (64, 2 * TOK), 0)
        pick = (row == group).astype(jnp.float32).astype(jnp.bfloat16)
        here = lax.dot_general(seen, pick, (((0,), (0,)), ((), ())), preferred_element_type=jnp.float32)
        allow = (row == group) | ((row < group) & (here > 0.5))
        bias[...] = jnp.where(allow, 0.0, -BIG).reshape(16, 4, 2 * TOK)
        query = q_ref[slot]

        def step(j, state):
            row_max, row_total, acc = state
            keys = kv_ref[0, pl.ds(2 * j, 2)].reshape(512, HD)
            s = jnp.dot(keys, query, preferred_element_type=jnp.float32) * scale
            s = s.reshape(4, TOK, 2 * TOK) + bias[j].reshape(4, 1, 2 * TOK)
            new_max = jnp.maximum(row_max, jnp.max(jnp.max(s, axis=0), axis=0, keepdims=True))
            keep = jnp.exp2(row_max - new_max)
            probs = jnp.exp2(s - new_max.reshape(1, 1, 2 * TOK))
            row_total = row_total * keep + jnp.sum(jnp.sum(probs, axis=0), axis=0, keepdims=True)
            probs = probs.astype(jnp.bfloat16).reshape(512, 2 * TOK)
            values = jnp.concatenate(
                [kv_ref[1, 2 * j + b, g * TOK : (g + 1) * TOK, :] for b in range(2) for g in range(2)], axis=1
            )
            acc = acc * keep + jnp.dot(values, probs, preferred_element_type=jnp.float32)
            return new_max, row_total, acc

        state = (
            jnp.full((1, 2 * TOK), -BIG, jnp.float32),
            jnp.zeros((1, 2 * TOK), jnp.float32),
            jnp.zeros((HD, 2 * TOK), jnp.float32),
        )
        row_max, row_total, acc = lax.fori_loop(0, (pair + 2) // 2, step, state)
        mixed = acc / row_total
        for g in range(2):
            o_ref[slot, g] = mixed[:, g * TOK : (g + 1) * TOK].T.astype(jnp.bfloat16)
        return carry

    slots = jnp.where(extra, 4, jnp.where(rank >= 4, 6, 5))
    lax.fori_loop(0, slots, one_slot, 0)


def project_kernel(
    o_ref, w_ref, hid_ref, gate_ref, inc_ref, out_ref, att, w, s1, r1, s2, r2, hs, gs,
    wsem, osend, orecv, send1, recv1, send2, recv2, hsend, hrecv
):
    y, z, x, c = coords()
    p = y * NZ + z
    hd = 2 * x + c
    extra, size, rank, half, head = team()
    wcopy = pltpu.make_async_copy(w_ref, w, wsem)
    wcopy.start()

    shift = [
        remote(hid_ref.at[pl.ds(0, TOK)], hs, hsend.at[0], hrecv.at[0], p - 1, hd),
        remote(gate_ref.at[0], gs, hsend.at[1], hrecv.at[1], p - 1, hd),
    ]

    @pl.when(p > 0)
    def _():
        for copy in shift:
            copy.start()

    def o_args(slot, g):
        pair = pair_of(slot, size, rank)
        pd = pair - 1 + g
        dst = att.at[pl.ds((1 - g) * TOK, TOK), pl.ds(pl.multiple_of(head * HD, HD), HD)]
        return o_ref.at[slot, g], dst, osend.at[2 * slot + g], orecv.at[(1 - g) * LOCAL_HEADS + head], pd, 2 * x + half

    for slot in range(SLOTS):
        for g in range(2):
            src, dst, send, recv, pd, hdd = o_args(slot, g)
            me = jnp.logical_and(pd == p, hdd == hd)

            @pl.when(jnp.logical_and(pd >= 0, me))
            def _():
                pltpu.make_async_copy(src, dst, recv).start()

            @pl.when(jnp.logical_and(pd >= 0, jnp.logical_not(me)))
            def _():
                remote(src, dst, send, recv, pd, hdd).start()

    last = p == PAIRS - 1

    @pl.when(last)
    def _():
        att[TOK:, :] = jnp.zeros((TOK, LOCAL_HEADS * HD), jnp.bfloat16)

    def o_arrive(g, h):
        dst = att.at[pl.ds(g * TOK, TOK), pl.ds(h * HD, HD)]
        remote(dst, dst, osend.at[0], orecv.at[g * LOCAL_HEADS + h], p, hd).wait_recv()

    for h in range(LOCAL_HEADS):
        o_arrive(0, h)

    @pl.when(jnp.logical_not(last))
    def _():
        for h in range(LOCAL_HEADS):
            o_arrive(1, h)

    wcopy.wait()
    width = LOCAL_HEADS * HD
    offsets = (2, 1, 3, 0)

    def part(j, core):
        xd = (x + offsets[j]) % NX
        cols = pl.ds(pl.multiple_of((2 * xd + core) * width, HD), width)
        return jnp.dot(att[...], w[:, cols], preferred_element_type=jnp.float32)

    def across(j):
        return remote(s1.at[j], r1.at[j], send1.at[j], recv1.at[j], p, 2 * x + 1 - c)

    def along(j):
        xd = (x + offsets[j]) % NX
        return remote(s2.at[j], r2.at[j], send2.at[j], recv2.at[j], p, 2 * xd + c)

    for j in range(4):
        s1[j] = part(j, 1 - c).astype(jnp.bfloat16)
        across(j).start()
    for j in range(4):
        mine = part(j, c)
        across(j).wait_recv()
        mine = mine + r1[j].astype(jnp.float32)
        if j < 3:
            s2[j] = mine.astype(jnp.bfloat16)
            along(j).start()
    total = mine
    for j in (1, 2, 0):
        along(j).wait_recv()
        total = total + r2[j].astype(jnp.float32)

    out_ref[:TOK, :] = (hid_ref[TOK:, :].astype(jnp.float32) + gate_ref[1, 0:1, :] * total[:TOK]).astype(jnp.bfloat16)

    @pl.when(last)
    def _():
        out_ref[TOK:, :] = inc_ref[...]

    @pl.when(jnp.logical_not(last))
    def _():
        for copy in shift:
            copy.wait_recv()
        out_ref[TOK:, :] = (hs[...].astype(jnp.float32) + gs[0:1, :] * total[TOK:]).astype(jnp.bfloat16)

    @pl.when(p > 0)
    def _():
        for copy in shift:
            copy.wait_send()

    for j in range(4):
        across(j).wait_send()
        if j < 3:
            along(j).wait_send()
    for slot in range(SLOTS):
        for g in range(2):
            src, dst, send, recv, pd, hdd = o_args(slot, g)
            me = jnp.logical_and(pd == p, hdd == hd)

            @pl.when(jnp.logical_and(pd >= 0, jnp.logical_not(me)))
            def _():
                remote(src, dst, send, recv, pd, hdd).wait_send()


def on_device(query_states, key_states, value_states, hidden, out_weight, gate_table, levels, visible, incoming):
    dma = pltpu.SemaphoreType.DMA
    bf16 = jnp.bfloat16
    width = LOCAL_HEADS * HD
    rows = 2 * TOK
    kv, queries = pl.pallas_call(
        gather_kernel,
        out_shape=(
            jax.ShapeDtypeStruct((3, PAIRS, rows, HD), bf16),
            jax.ShapeDtypeStruct((SLOTS, HD, rows), bf16),
        ),
        in_specs=[VMEM] * 3,
        out_specs=(VMEM, VMEM),
        scratch_shapes=[
            pltpu.VMEM((LOCAL_HEADS, HD, rows), bf16),
            pltpu.VMEM((LOCAL_HEADS, rows, HD), bf16),
            dma((5,)),
            dma((5,)),
            dma((5,)),
            dma((SLOTS,)),
            dma((PAIRS,)),
            dma((PAIRS,)),
            dma((PAIRS,)),
            dma((12,)),
            dma((12,)),
            dma((12,)),
            dma((12,)),
            dma((PAIRS,)),
        ],
        compiler_params=pltpu.CompilerParams(has_side_effects=True, vmem_limit_bytes=40 << 20),
        name="gather",
    )(query_states, key_states, value_states)

    attended = pl.pallas_call(
        attend_kernel,
        out_shape=jax.ShapeDtypeStruct((SLOTS, 2, TOK, HD), bf16),
        grid=(1,),
        in_specs=[
            pl.BlockSpec((2, PAIRS, rows, HD), lambda i: (0, 0, 0, 0)),
            pl.BlockSpec((SLOTS, HD, rows), lambda i: (0, 0, 0)),
            pl.BlockSpec((64, 64), lambda i: (0, 0)),
        ],
        out_specs=pl.BlockSpec((SLOTS, 2, TOK, HD), lambda i: (0, 0, 0, 0)),
        scratch_shapes=[pltpu.VMEM((16, 4, rows), jnp.float32)],
        compiler_params=pltpu.CompilerParams(vmem_limit_bytes=40 << 20),
        name="attend",
    )(kv, queries, visible)

    gates = jnp.concatenate([lax.dynamic_slice_in_dim(gate_table, levels[g], 1, 0) for g in range(2)], axis=0)
    gates = jnp.broadcast_to(gates[:, None, :], (2, 8, width))
    return pl.pallas_call(
        project_kernel,
        out_shape=jax.ShapeDtypeStruct((rows, width), bf16),
        in_specs=[VMEM, ANY, VMEM, VMEM, VMEM],
        out_specs=VMEM,
        scratch_shapes=[
            pltpu.VMEM((rows, width), bf16),
            pltpu.VMEM((width, 8 * width), bf16),
            pltpu.VMEM((4, rows, width), bf16),
            pltpu.VMEM((4, rows, width), bf16),
            pltpu.VMEM((3, rows, width), bf16),
            pltpu.VMEM((3, rows, width), bf16),
            pltpu.VMEM((TOK, width), bf16),
            pltpu.VMEM((8, width), jnp.float32),
            dma(()),
            dma((2 * SLOTS,)),
            dma((2 * LOCAL_HEADS,)),
            dma((4,)),
            dma((4,)),
            dma((3,)),
            dma((3,)),
            dma((2,)),
            dma((2,)),
        ],
        compiler_params=pltpu.CompilerParams(has_side_effects=True, vmem_limit_bytes=40 << 20),
        name="project",
    )(attended, out_weight, hidden, gates, incoming)


def solution(mesh):
    return jax.shard_map(
        on_device,
        mesh=mesh,
        in_specs=(
            P("group", "head"),
            P("group", "head"),
            P("group", "head"),
            P("group", "head"),
            P("head", None),
            P(None, "head"),
            P("group"),
            P(),
            P(None, "head"),
        ),
        out_specs=P("group", "head"),
        check_vma=False,
    )
```

time: 422 us -> 156 us (0.37); the launches traced: 416 us -> 155 us
  waiting for transfers between devices: 348 us -> 0 us
  Pallas kernels: 0 us -> 143 us
  other arithmetic: 14 us -> 0.01 us
  matrix products: 11.1 us -> 0 us
  loops' own time: 11.1 us -> 0 us
  between operations: 13.2 us -> 3.92 us
  local copies, waits for them, and re-layouts: 17.7 us -> 8.68 us
    all_gather x2 -> x0, waiting for transfers between devices: 227 us -> none  [the longest x1 115 us: on_device(): lax.all_gather(value_states, 'group', axis=0, tiled=True)]
    pallas_call x0 -> x3, Pallas kernels: none -> 143 us  [the longest x1 78.8 us: on_device(): pl.pallas_call(gather_kernel, out_shape=(jax.ShapeDtypeStruct((3, PAIRS,...]
    unnamed x4 -> x0, waiting for transfers between devices: 115 us -> none
    reduce_or x16 -> x0, other arithmetic: 12.3 us -> none  [block_attend(): return lax.cond(jnp.any(allowed_group), compute, unchanged, state)]
    another operation x17 -> x0, loops' own time: 11.1 us -> none  [the longest x1 10.8 us: fold_rows(): return lax.fori_loop(0, block_count, one_block, state)]
    dot_general x4 -> x0, matrix products: 11.1 us -> none  [the longest x1 6.61 us: on_device(): jnp.dot(attended, out_weight, preferred_element_type=jnp.float32)]
    ppermute x1 -> x0, waiting for transfers between devices: 4.76 us -> none  [from_behind(): return lax.ppermute(shard, axis, pairs)]
    unnamed x13 -> x17, local copies, waits for them, and re-layouts: 11.4 us -> 7.31 us
  transfers between devices with their start and end apart: 4 -> 0, of which waited for: 4 -> 0; matrix products, arithmetic and copies ran while one was open for 1% -> 0% of each run, Pallas kernels for 0% -> 0%
where the time goes in v1:
time: 156 us; the launch traced here: 155 us
  Pallas kernels  143 us (92%)
  local copies, waits for them, and re-layouts  8.68 us (6%)
  between operations  3.92 us (3%)
    pallas_call x1, Pallas kernels, on_device(): pl.pallas_call(gather_kernel, out_shape=(jax.ShapeDtypeStruct((3, PAIRS,...  78.8 us
    pallas_call x1, Pallas kernels, on_device(): pl.pallas_call(project_kernel, out_shape=jax.ShapeDtypeStruct((rows, widt...  45.3 us
    pallas_call x1, Pallas kernels, on_device(): pl.pallas_call(attend_kernel, out_shape=jax.ShapeDtypeStruct((SLOTS, 2, T...  18.7 us
    unnamed x17, local copies, waits for them, and re-layouts  7.31 us

profile of v1, /device:TPU:1, one launch (start us, length us, event | category | flops | bytes accessed | tf_op | source)
XLA Modules:
  0.0 155.4 jit_solution(4679358523425574473)
XLA Ops:
  0.0 0.0 copy-start.1
  0.0 0.0 copy-start.2
  0.0 1.0 copy-done.2
  1.0 0.0 copy-start.3
  1.0 1.0 copy-done.3
  2.0 0.0 copy-start.4
  2.0 1.0 copy-done.4
  3.0 0.0 copy-start.7
  3.0 0.0 copy-start.5
  3.0 78.8 %gather.1 = (bf16[3,32,256,128]{3,2,1,0:T(8,128)(2,1)S(1)}, bf16[6,128,256]{2,1,0:T(8,128)(2,1)S(1)}) custom-call(bf16[256,640]{1,0:T(8,128)(2,1)S(1)} %copy-done.2, bf16[256,640]{1,0:T(8,128)(2,1)S(1)} %copy-done.3, bf16[256,640]{1,0:T(8,128)(2,1)S(1)} %copy-done.4), custom_call_target="tpu_custom_call" | custom-call | tf_op jit(solution)/shard_map/gather/pallas_call | solution.py:393
  81.8 0.0 copy-start.6
  81.8 0.7 copy-done.6
  82.5 18.7 %attend.1.o_ref = bf16[6,2,128,128]{3,2,1,0:T(8,128)(2,1)S(1)} custom-call(bf16[3,32,256,128]{3,2,1,0:T(8,128)(2,1)S(1)} %get-tuple-element.7.kv_ref, bf16[6,128,256]{2,1,0:T(8,128)(2,1)S(1)} %get-tuple-element.8.q_ref, s32[64,64]{1,0:T(8,128)S(1)} %copy-done.6), custom_call_target="tpu_custom_call" | custom-call | tf_op jit(solution)/shard_map/attend/pallas_call | solution.py:421
  101.2 0.0 copy-done.7
  101.2 0.6 fusion
  105.7 0.8 constant_dynamic-slice_fusion.1
  106.5 0.0 copy-done.1
  106.5 0.0 copy-done.5
  106.5 0.0 copy-start
  106.5 2.9 %copy-done = bf16[640,5120]{1,0:T(8,128)(2,1)S(1)} copy-done((bf16[640,5120]{1,0:T(8,128)(2,1)S(1)}, bf16[640,5120]{1,0:T(8,128)(2,1)}, u32[]{:S(2)}) %copy-start) | copy-done | bytes 6553624
  109.3 45.3 %project.1 = bf16[256,640]{1,0:T(8,128)(2,1)S(1)} custom-call(bf16[6,2,128,128]{3,2,1,0:T(8,128)(2,1)S(1)} %attend.1.o_ref, bf16[640,5120]{1,0:T(8,128)(2,1)S(1)} %copy-done, bf16[256,640]{1,0:T(8,128)(2,1)S(1)} %copy-done.1, f32[2,8,640]{2,1,0:T(8,128)S(1)} %broadcast_in_dim.2.gate_ref, bf16[128,640]{1,0:T(8,128)(2,1)S(1)} %copy-done.5), custom_call_target="tpu_custom_call" | custom-call | tf_op jit(solution)/shard_map/project/pallas_call | solution.py:438
  154.7 0.7 copy.11
  (2 shorter events, 0.0 us)
Async XLA Ops:
  0.0 106.5 %copy-start.1 = (bf16[256,640]{1,0:T(8,128)(2,1)S(1)}, bf16[256,640]{1,0:T(8,128)(2,1)}, u32[]{:S(2)}) copy-start(bf16[256,640]{1,0:T(8,128)(2,1)} %hid_ref.1) | copy-start | bytes 983044
  0.0 1.0 copy-start.2
  1.0 1.0 copy-start.3
  2.0 1.0 copy-start.4
  3.0 98.3 %copy-start.7 = (s32[2]{0:T(128)S(1)}, s32[2]{0:T(128)}, u32[]{:S(2)}) copy-start(s32[2]{0:T(128)} %param.15) | copy-start | bytes 28
  3.0 103.5 %copy-start.5 = (bf16[128,640]{1,0:T(8,128)(2,1)S(1)}, bf16[128,640]{1,0:T(8,128)(2,1)}, u32[]{:S(2)}) copy-start(bf16[128,640]{1,0:T(8,128)(2,1)} %inc_ref.1) | copy-start | bytes 491524
  81.8 0.8 copy-start.6
  106.5 2.9 %copy-start = (bf16[640,5120]{1,0:T(8,128)(2,1)S(1)}, bf16[640,5120]{1,0:T(8,128)(2,1)}, u32[]{:S(2)}) copy-start(bf16[640,5120]{1,0:T(8,128)(2,1)} %w_ref.1) | copy-start | bytes 19660804

commit v2 on v0

v2 whole, which is shorter than its diff:
```python
import math

import jax
import jax.numpy as jnp
from jax import lax
from jax.experimental import pallas as pl
from jax.experimental.pallas import tpu as pltpu
from jax.sharding import PartitionSpec as P

HD = 128
TOK = 128
ROWS = 2 * TOK
NY, NZ, NX = 4, 8, 4
PAIRS = NY * NZ
HEADS = 5
WIDTH = HEADS * HD
LEVELS = 1000
MAIN_TEAM, EXTRA_TEAM = 6, 8
SLOTS = 6
CHUNK = 4
KEYS = CHUNK * ROWS
PARTS = 2 * CHUNK
PER_QUARTER = NZ // CHUNK
MASKED = -1e30
LOWEST = -1e20
MESH = pl.DeviceIdType.MESH
ANY = pl.BlockSpec(memory_space=pl.ANY)
bf16 = jnp.bfloat16
f32 = jnp.float32


def remote(src, dst, send, recv, p, hd):
    return pltpu.make_async_remote_copy(
        src_ref=src, dst_ref=dst, send_sem=send, recv_sem=recv, device_id=(p, hd), device_id_type=MESH
    )


def unless(cond):
    return pl.when(jnp.logical_not(cond))


def pair_of(slot, size, rank):
    pos = jnp.where(slot % 2 == 0, rank, size - 1 - rank)
    return PAIRS - 1 - (slot * size + pos)


def owner_of(pair, head, x, c):
    size = MAIN_TEAM if head < 4 else EXTRA_TEAM
    t = PAIRS - 1 - pair
    slot = t // size
    pos = t % size
    rank = jnp.where(slot % 2 == 0, pos, size - 1 - pos)
    chip = rank // 2
    if head < 4:
        return ((x + 1 + chip) % NY) * NZ + 4 * c + head, 2 * x + rank % 2, slot
    return chip * NZ + 2 * x + c, 2 * chip + rank % 2, slot


def body(
    q_hbm, k_hbm, v_hbm, hid_hbm, w_hbm, gate_hbm, levels, vis_hbm, inc_hbm, out_ref,
    q_in, k_in, v_in, hid, w, gate, vis, inc, buf, qbuf, qt, vt, bias, s_a, s_b, p_a, p_b, keep_a, keep_b,
    row_max, acc, o_buf, att, s1, r1, far, far_in, near, near_in, hs, gs, gs_out,
    lsem, qsend, ksend, vsend, qrecv, rmain, rextra, rsib, snext, sprev, enext, eprev, ssib,
    osend, orecv, send1, recv1, fsend, frecv, nsend, nrecv, hsend, hrecv
):
    p = lax.axis_index("group")
    hd = lax.axis_index("head")
    y, z, x, c = p // NZ, p % NZ, hd // 2, hd % 2
    sib = 2 * x + 1 - c
    half, col = z // 4, z % 4
    extra = y == x
    last = p == PAIRS - 1
    size = jnp.where(extra, EXTRA_TEAM, MAIN_TEAM)
    rank = jnp.where(extra, 2 * x + c, 2 * ((y - x - 1 + NY) % NY) + c)
    head = jnp.where(extra, 4, col)
    home = jnp.where(extra, z, 2 * x + half)
    pairs = [pair_of(slot, size, rank) for slot in range(SLOTS)]
    yn, yp, yo = (y + 1) % NY, (y + 3) % NY, (y + 2) % NY

    def is_me(pd, hdd):
        return jnp.logical_and(pd == p, hdd == hd)

    loads = [
        pltpu.make_async_copy(src, dst, lsem.at[i])
        for i, (src, dst) in enumerate(
            [(k_hbm, k_in), (v_hbm, v_in), (q_hbm, q_in), (hid_hbm, hid), (vis_hbm, vis), (gate_hbm, gate), (w_hbm, w), (inc_hbm, inc)]
        )
    ]
    for copy in loads:
        copy.start()

    barrier = pltpu.get_barrier_semaphore()

    def ready(pd, hdd):
        pl.semaphore_signal(barrier, inc=1, device_id=(pd, hdd), device_id_type=MESH)

    def ready_unless_me(pd, hdd):
        @unless(is_me(pd, hdd))
        def _():
            ready(pd, hdd)

    for dz in range(NZ):
        ready_unless_me(y * NZ + dz, 2 * x + half)
    ready(yn * NZ + z, hd)
    ready(yp * NZ + z, hd)
    ready(p, sib)

    @pl.when(extra)
    def _():
        for dz in range(NZ):
            ready_unless_me(y * NZ + dz, z)
        ready(yn * NZ + z, 2 * yn + c)
        ready(yp * NZ + z, 2 * yp + c)

    for slot in range(SLOTS):

        @pl.when(pairs[slot] >= 0)
        def _():
            ready_unless_me(pairs[slot], home)

    for h in range(HEADS):
        pd, hdd, _ = owner_of(p, h, x, c)
        ready_unless_me(pd, hdd)

    @unless(last)
    def _():
        for h in range(HEADS):
            pd, hdd, _ = owner_of(p + 1, h, x, c)
            ready_unless_me(pd, hdd)
        ready(p + 1, hd)

    xn, xp, xo = (x + 1) % NX, (x + 3) % NX, (x + 2) % NX
    ready(p, 2 * xn + c)
    ready(p, 2 * xp + c)

    def count(flag):
        return flag.astype(jnp.int32)

    def others(pd, hdd):
        return 1 - count(is_me(pd, hdd))

    expected = 2 + 1 + 2 + jnp.where(extra, 2, 0) + count(p > 0)
    for k in range(2):
        for h in range(4):
            expected = expected + others(y * NZ + 4 * c + h, 2 * x + k)
        expected = expected + others(y * NZ + hd, 2 * y + k)
    for h in range(HEADS):
        pd, hdd, _ = owner_of(p, h, x, c)
        expected = expected + others(pd, hdd)
    for slot in range(SLOTS):
        for g in range(2):
            expected = expected + jnp.where(pairs[slot] - 1 + g >= 0, others(pairs[slot] - 1 + g, home), 0)

    def put(src, dst, send, recv, pd, hdd):
        @pl.when(is_me(pd, hdd))
        def _():
            pltpu.make_async_copy(src, dst, recv).start()

        @unless(is_me(pd, hdd))
        def _():
            remote(src, dst, send, recv, pd, hdd).start()

    def put_done(src, dst, send, recv, pd, hdd):
        @unless(is_me(pd, hdd))
        def _():
            remote(src, dst, send, recv, pd, hdd).wait_send()

    def kv_args(h, k):
        src = k_in.at[:, pl.ds(h * HD, HD)] if k == 0 else vt.at[h]
        send = ksend.at[h] if k == 0 else vsend.at[h]
        if h < 4:
            return src, buf.at[jnp.where(y == x, 2, k), p], send, rmain.at[p], y * NZ + 4 * c + h, 2 * x + k
        return src, buf.at[k, p], send, rextra.at[p], y * NZ + hd, 2 * y + k

    def q_args(h):
        pd, hdd, slot = owner_of(p, h, x, c)
        return qt.at[h], qbuf.at[slot], qsend.at[h], qrecv.at[slot], pd, hdd

    for i in range(3):
        loads[i].wait()
    for h in range(HEADS):
        for g in range(2):
            vt[h, g * TOK : (g + 1) * TOK, :] = v_in[g * TOK : (g + 1) * TOK, h * HD : (h + 1) * HD].T
        qt[h] = q_in[:, h * HD : (h + 1) * HD].T
    for slot in range(3, SLOTS):

        @pl.when(pairs[slot] < 0)
        def _():
            qbuf[slot] = jnp.zeros((HD, ROWS), bf16)

    @pl.when(last)
    def _():
        att[TOK:, :] = jnp.zeros((TOK, WIDTH), bf16)

    pl.semaphore_wait(barrier, expected)

    for h in range(HEADS):
        for k in range(2):
            put(*kv_args(h, k))
    for h in range(HEADS):
        put(*q_args(h))

    for i in range(3, 6):
        loads[i].wait()
    gs_out[...] = jnp.broadcast_to(gate[pl.ds(levels[0], 1), :], (8, WIDTH))
    shift = [
        remote(hid.at[pl.ds(0, TOK)], hs, hsend.at[0], hrecv.at[0], p - 1, hd),
        remote(gs_out, gs, hsend.at[1], hrecv.at[1], p - 1, hd),
    ]

    @pl.when(p > 0)
    def _():
        for copy in shift:
            copy.start()

    seen = (vis[...] == 1).astype(f32).astype(bf16)
    key_group = lax.broadcasted_iota(jnp.int32, (64, ROWS), 0)
    second = (lax.broadcasted_iota(jnp.int32, (64, ROWS), 1) >= TOK).astype(jnp.int32)
    for slot in range(SLOTS):
        group = 2 * pairs[slot] + second
        pick = (key_group == group).astype(f32).astype(bf16)
        here = lax.dot_general(seen, pick, (((0,), (0,)), ((), ())), preferred_element_type=f32)
        allow = (key_group == group) | ((key_group < group) & (here > 0.5))
        bias[slot] = jnp.where(allow, 0.0, MASKED).reshape(PAIRS // CHUNK, PARTS, ROWS)
        row_max[slot] = jnp.full((8, ROWS), LOWEST, f32)
        acc[slot] = jnp.zeros((HD + 16, ROWS), f32)

    def sibling(i):
        return remote(buf.at[c, i], buf.at[c, i], ssib.at[i], rsib.at[i], p, sib)

    def ring(step, main):
        if main:
            mine = jnp.where(extra, 2, c)
            there_n, there_p = jnp.where(yn == x, 2, c), jnp.where(yp == x, 2, c)
            hn, hp = hd, hd
            sems, to_next, to_prev = rmain, snext, sprev
        else:
            mine, there_n, there_p = c, c, c
            hn, hp = 2 * yn + c, 2 * yp + c
            sems, to_next, to_prev = rextra, enext, eprev
        pn, pp = yn * NZ + z, yp * NZ + z

        def arrive(i):
            remote(buf.at[mine, i], buf.at[mine, i], to_next.at[0], sems.at[i], pn, hn).wait_recv()

        def go_next(i, s):
            return remote(buf.at[mine, i], buf.at[there_n, i], to_next.at[s], sems.at[i], pn, hn)

        def go_prev(i, s):
            return remote(buf.at[mine, i], buf.at[there_p, i], to_prev.at[s], sems.at[i], pp, hp)

        def across(i):
            if main:

                @unless(extra)
                def _():
                    sibling(i).start()
            else:
                sibling(i).start()

        def own(b, carry):
            i = y * NZ + b
            arrive(i)
            go_next(i, b).start()
            go_prev(i, b).start()
            across(i)
            return carry

        def forward(b, carry):
            i = yp * NZ + b
            arrive(i)
            go_next(i, 8 + b).start()
            across(i)
            i = yn * NZ + 4 + b
            arrive(i)
            go_prev(i, 8 + b).start()
            across(i)
            return carry

        def rest(b, carry):
            for i in (yp * NZ + 4 + b, yn * NZ + b):
                arrive(i)
                across(i)
            return carry

        def far_side(b, carry):
            i = yo * NZ + b
            arrive(i)
            across(i)
            return carry

        def close(b, carry):
            go_next(b, b).wait_send()
            go_prev(b, b).wait_send()
            return carry

        if step == 0:
            lax.fori_loop(0, NZ, own, 0)
        elif step == 1:
            lax.fori_loop(0, 4, forward, 0)
        elif step == 2:
            lax.fori_loop(0, 4, rest, 0)
        elif step == 3:
            lax.fori_loop(0, NZ, far_side, 0)
        else:
            lax.fori_loop(0, 12, close, 0)

    def rings(step):
        ring(step, True)

        @pl.when(extra)
        def _():
            ring(step, False)

    def from_sibling(quarter):
        def one(b, carry):
            i = quarter * NZ + b
            remote(buf.at[1 - c, i], buf.at[1 - c, i], ssib.at[i], rsib.at[i], p, sib).wait_recv()
            return carry

        lax.fori_loop(0, NZ, one, 0)

    ones = jnp.ones((16, KEYS), bf16)
    scale = math.log2(math.e) / math.sqrt(HD)

    def attend(quarter):
        ends = []
        total = 0
        for slot in range(SLOTS):
            total = total + jnp.clip((pairs[slot] + 1 - NZ * quarter + CHUNK - 1) // CHUNK, 0, PER_QUARTER)
            ends.append(total)

        def item(i):
            slot, base = 0, 0
            for s in range(SLOTS - 1):
                past = i >= ends[s]
                slot = slot + past.astype(jnp.int32)
                base = jnp.where(past, ends[s], base)
            return slot, quarter * PER_QUARTER + jnp.clip(i - base, 0, PER_QUARTER - 1), i < total

        def score(i, s):
            slot, chunk, _ = item(i)
            keys = buf[0, pl.ds(CHUNK * chunk, CHUNK)].reshape(KEYS, HD)
            s[...] = jnp.dot(keys, qbuf[slot], preferred_element_type=f32)

        def weigh(i, probs, keep):
            slot, chunk, _ = item(i)
            values = jnp.concatenate(
                [buf[1, CHUNK * chunk + b, g * TOK : (g + 1) * TOK, :] for b in range(CHUNK) for g in range(2)], axis=1
            )
            values = jnp.concatenate([values, ones], axis=0)
            acc[slot] = acc[slot] * keep[0:1] + jnp.dot(values, probs[...], preferred_element_type=f32)

        def soften(i, s, probs, keep):
            slot, chunk, valid = item(i)
            offset = bias[slot, chunk] + jnp.where(valid, 0.0, MASKED)
            old = row_max[slot, 0:1]
            new = old
            for g in range(PARTS):
                top = jnp.max(s[g * TOK : (g + 1) * TOK, :], axis=0, keepdims=True)
                new = jnp.maximum(new, top * scale + offset[g : g + 1])
            keep[...] = jnp.broadcast_to(jnp.exp2(old - new), (8, ROWS))
            row_max[slot] = jnp.broadcast_to(new, (8, ROWS))
            for g in range(PARTS):
                t = s[g * TOK : (g + 1) * TOK, :] * scale + (offset[g : g + 1] - new)
                probs[g * TOK : (g + 1) * TOK, :] = jnp.exp2(t).astype(bf16)

        score(0, s_a)
        p_b[...] = jnp.zeros_like(p_b)
        keep_b[...] = jnp.ones_like(keep_b)

        def two(n, carry):
            i = 2 * n
            weigh(jnp.maximum(i - 1, 0), p_b, keep_b)
            score(i + 1, s_b)
            soften(i, s_a, p_a, keep_a)
            weigh(i, p_a, keep_a)
            score(i + 2, s_a)
            soften(i + 1, s_b, p_b, keep_b)
            return carry

        turns = (total + 1) // 2
        lax.fori_loop(0, turns, two, 0)

        @pl.when(turns > 0)
        def _():
            weigh(2 * turns - 1, p_b, keep_b)

    rings(0)
    rings(1)
    from_sibling(y)
    for slot in range(SLOTS):

        @pl.when(pairs[slot] >= 0)
        def _():
            remote(qt.at[0], qbuf.at[slot], qsend.at[0], qrecv.at[slot], p, hd).wait_recv()

    attend(y)
    rings(2)
    from_sibling(yp)
    attend(yp)
    from_sibling(yn)
    attend(yn)
    rings(3)
    from_sibling(yo)
    attend(yo)

    def o_args(slot, g):
        pd = pairs[slot] - 1 + g
        dst = att.at[pl.ds((1 - g) * TOK, TOK), pl.ds(pl.multiple_of(head * HD, HD), HD)]
        return o_buf.at[slot, g], dst, osend.at[2 * slot + g], orecv.at[(1 - g) * HEADS + head], pd, home

    for slot in range(SLOTS):

        @pl.when(pairs[slot] >= 0)
        def _():
            mixed = acc[slot, :HD] / acc[slot, HD : HD + 1]
            for g in range(2):
                o_buf[slot, g] = mixed[:, g * TOK : (g + 1) * TOK].T.astype(bf16)
            put(*o_args(slot, 1))

        @pl.when(pairs[slot] >= 1)
        def _():
            put(*o_args(slot, 0))

    def o_arrive(g):
        for h in range(HEADS):
            dst = att.at[pl.ds(g * TOK, TOK), pl.ds(h * HD, HD)]
            remote(dst, dst, osend.at[0], orecv.at[g * HEADS + h], p, hd).wait_recv()

    o_arrive(0)

    @unless(last)
    def _():
        o_arrive(1)

    loads[6].wait()
    loads[7].wait()

    def part(xd, core):
        cols = pl.ds(pl.multiple_of((2 * xd + core) * WIDTH, HD), WIDTH)
        return jnp.dot(att[...], w[:, cols], preferred_element_type=f32)

    turn = (xo, xn, xp, x)

    def over(j):
        return remote(s1.at[j], r1.at[j], send1.at[j], recv1.at[j], p, sib)

    def far_copy(d):
        return remote(far.at[pl.ds(d * TOK, TOK)], far_in.at[d], fsend.at[d], frecv.at[d], p, 2 * (xn, xp)[d] + c)

    def near_copy(d):
        return remote(near.at[d], near_in.at[d], nsend.at[d], nrecv.at[d], p, 2 * (xn, xp)[d] + c)

    for j in range(4):
        s1[j] = part(turn[j], 1 - c).astype(bf16)
        over(j).start()

    def both(j):
        mine = part(turn[j], c)
        over(j).wait_recv()
        return mine + r1[j].astype(f32)

    far[...] = both(0).astype(bf16)
    far_copy(0).start()
    far_copy(1).start()
    for d in range(2):
        mine = both(1 + d)
        far_copy(d).wait_recv()
        near[d, (1 - d) * TOK : (2 - d) * TOK] = mine[(1 - d) * TOK : (2 - d) * TOK].astype(bf16)
        rows = slice(d * TOK, (d + 1) * TOK)
        near[d, rows] = (mine[rows] + far_in[d].astype(f32)).astype(bf16)
        near_copy(d).start()
    summed = both(3)
    for d in range(2):
        near_copy(d).wait_recv()
        summed = summed + near_in[d].astype(f32)

    out_ref[:TOK, :] = (hid[TOK:, :].astype(f32) + gate[pl.ds(levels[1], 1), :] * summed[:TOK]).astype(bf16)

    @pl.when(last)
    def _():
        out_ref[TOK:, :] = inc[...]

    @unless(last)
    def _():
        for copy in shift:
            copy.wait_recv()
        out_ref[TOK:, :] = (hs[...].astype(f32) + gs[0:1, :] * summed[TOK:]).astype(bf16)

    @pl.when(p > 0)
    def _():
        for copy in shift:
            copy.wait_send()

    for h in range(HEADS):
        for k in range(2):
            put_done(*kv_args(h, k))
        put_done(*q_args(h))
    rings(4)

    def sibling_done(i, carry):
        sibling(i).wait_send()
        return carry

    lax.fori_loop(0, PAIRS, sibling_done, 0)
    for slot in range(SLOTS):

        @pl.when(pairs[slot] >= 0)
        def _():
            put_done(*o_args(slot, 1))

        @pl.when(pairs[slot] >= 1)
        def _():
            put_done(*o_args(slot, 0))

    for j in range(4):
        over(j).wait_send()
    for d in range(2):
        far_copy(d).wait_send()
        near_copy(d).wait_send()


def on_device(query_states, key_states, value_states, hidden, out_weight, gate_table, levels, visible, incoming):
    dma = pltpu.SemaphoreType.DMA
    vmem = pltpu.VMEM
    return pl.pallas_call(
        body,
        out_shape=jax.ShapeDtypeStruct((ROWS, WIDTH), bf16),
        in_specs=[ANY] * 6 + [pl.BlockSpec(memory_space=pltpu.SMEM)] + [ANY] * 2,
        out_specs=pl.BlockSpec(memory_space=pltpu.VMEM),
        scratch_shapes=[
            vmem((ROWS, WIDTH), bf16),
            vmem((ROWS, WIDTH), bf16),
            vmem((ROWS, WIDTH), bf16),
            vmem((ROWS, WIDTH), bf16),
            vmem((WIDTH, 8 * WIDTH), bf16),
            vmem((LEVELS, WIDTH), f32),
            vmem((64, 64), jnp.int32),
            vmem((TOK, WIDTH), bf16),
            vmem((3, PAIRS, ROWS, HD), bf16),
            vmem((SLOTS, HD, ROWS), bf16),
            vmem((HEADS, HD, ROWS), bf16),
            vmem((HEADS, ROWS, HD), bf16),
            vmem((SLOTS, PAIRS // CHUNK, PARTS, ROWS), f32),
            vmem((KEYS, ROWS), f32),
            vmem((KEYS, ROWS), f32),
            vmem((KEYS, ROWS), bf16),
            vmem((KEYS, ROWS), bf16),
            vmem((8, ROWS), f32),
            vmem((8, ROWS), f32),
            vmem((SLOTS, 8, ROWS), f32),
            vmem((SLOTS, HD + 16, ROWS), f32),
            vmem((SLOTS, 2, TOK, HD), bf16),
            vmem((ROWS, WIDTH), bf16),
            vmem((4, ROWS, WIDTH), bf16),
            vmem((4, ROWS, WIDTH), bf16),
            vmem((ROWS, WIDTH), bf16),
            vmem((2, TOK, WIDTH), bf16),
            vmem((2, ROWS, WIDTH), bf16),
            vmem((2, ROWS, WIDTH), bf16),
            vmem((TOK, WIDTH), bf16),
            vmem((8, WIDTH), f32),
            vmem((8, WIDTH), f32),
            dma((8,)),
            dma((5,)),
            dma((5,)),
            dma((5,)),
            dma((SLOTS,)),
            dma((PAIRS,)),
            dma((PAIRS,)),
            dma((PAIRS,)),
            dma((12,)),
            dma((12,)),
            dma((12,)),
            dma((12,)),
            dma((PAIRS,)),
            dma((2 * SLOTS,)),
            dma((2 * HEADS,)),
            dma((4,)),
            dma((4,)),
            dma((2,)),
            dma((2,)),
            dma((2,)),
            dma((2,)),
            dma((2,)),
            dma((2,)),
        ],
        compiler_params=pltpu.CompilerParams(has_side_effects=True, collective_id=0, vmem_limit_bytes=56 << 20),
        name="block",
    )(query_states, key_states, value_states, hidden, out_weight, gate_table, levels, visible, incoming)


def solution(mesh):
    return jax.shard_map(
        on_device,
        mesh=mesh,
        in_specs=(
            P("group", "head"),
            P("group", "head"),
            P("group", "head"),
            P("group", "head"),
            P("head", None),
            P(None, "head"),
            P("group"),
            P(),
            P(None, "head"),
        ),
        out_specs=P("group", "head"),
        check_vma=False,
    )
```

time: 422 us -> 113 us (0.27)
  the two profiles are of different devices: /device:TPU:1 before, /device:TPU:102 now
where the time goes in v2:
time: 113 us; the launch traced here: 112 us
  Pallas kernels  111 us (98%)
  local copies, waits for them, and re-layouts  1.73 us (2%)
    pallas_call x1, Pallas kernels, on_device(): pl.pallas_call(body, out_shape=jax.ShapeDtypeStruct((ROWS, WIDTH), bf16),...  111 us

profile of v2, /device:TPU:102, one launch (start us, length us, event | category | flops | bytes accessed | tf_op | source)
XLA Modules:
  0.0 112.4 jit_solution(7581817831778395636)
XLA Ops:
  0.0 110.7 %block.1 = bf16[256,640]{1,0:T(8,128)(2,1)} custom-call(bf16[256,640]{1,0:T(8,128)(2,1)} %q_hbm.1, bf16[256,640]{1,0:T(8,128)(2,1)} %k_hbm.1, bf16[256,640]{1,0:T(8,128)(2,1)} %v_hbm.1, bf16[256,640]{1,0:T(8,128)(2,1)} %hid_hbm.1, bf16[640,5120]{1,0:T(8,128)(2,1)} %w_hbm.1, f32[1000,640]{1,0:T(8,128)} %gate_hbm.1, s32[2]{0:T(128)} %levels.1, ...), custom_call_target="tpu_custom_call" | custom-call | tf_op jit(solution)/shard_map/block/pallas_call | solution.py:527
  110.7 1.7 %copy.11 = bf16[256,640]{1,0:T(8,128)(2,1)} copy(bf16[256,640]{1,0:T(8,128)(2,1)} %block.1) | data formatting | bytes 655360

commit v3 on v2

--- a/solution.py
+++ b/solution.py
@@ -21,6 +21,7 @@
 KEYS = CHUNK * ROWS
 PARTS = 2 * CHUNK
 PER_QUARTER = NZ // CHUNK
+AHEAD = 4
 MASKED = -1e30
 LOWEST = -1e20
 MESH = pl.DeviceIdType.MESH
@@ -52,14 +53,14 @@
     rank = jnp.where(slot % 2 == 0, pos, size - 1 - pos)
     chip = rank // 2
     if head < 4:
-        return ((x + 1 + chip) % NY) * NZ + 4 * c + head, 2 * x + rank % 2, slot
-    return chip * NZ + 2 * x + c, 2 * chip + rank % 2, slot
+        return ((head + 1 + chip) % NY) * NZ + 4 * c + head, 2 * x + rank % 2, slot
+    return x * NZ + x + 4 * c, 2 * chip + rank % 2, slot
 
 
 def body(
     q_hbm, k_hbm, v_hbm, hid_hbm, w_hbm, gate_hbm, levels, vis_hbm, inc_hbm, out_ref,
     q_in, k_in, v_in, hid, w, gate, vis, inc, buf, qbuf, qt, vt, bias, s_a, s_b, p_a, p_b, keep_a, keep_b,
-    row_max, acc, o_buf, att, s1, r1, far, far_in, near, near_in, hs, gs, gs_out,
+    row_max, acc, o_buf, att, s1, r1, far, far_in, near, near_in, keep, hs, gs, gs_out,
     lsem, qsend, ksend, vsend, qrecv, rmain, rextra, rsib, snext, sprev, enext, eprev, ssib,
     osend, orecv, send1, recv1, fsend, frecv, nsend, nrecv, hsend, hrecv
 ):
@@ -68,14 +69,17 @@
     y, z, x, c = p // NZ, p % NZ, hd // 2, hd % 2
     sib = 2 * x + 1 - c
     half, col = z // 4, z % 4
-    extra = y == x
+    extra = y == col
     last = p == PAIRS - 1
     size = jnp.where(extra, EXTRA_TEAM, MAIN_TEAM)
-    rank = jnp.where(extra, 2 * x + c, 2 * ((y - x - 1 + NY) % NY) + c)
+    rank = jnp.where(extra, 2 * x + c, 2 * ((y - col - 1 + NY) % NY) + c)
     head = jnp.where(extra, 4, col)
-    home = jnp.where(extra, z, 2 * x + half)
+    home = jnp.where(extra, 2 * col, 2 * x) + half
     pairs = [pair_of(slot, size, rank) for slot in range(SLOTS)]
     yn, yp, yo = (y + 1) % NY, (y + 3) % NY, (y + 2) % NY
+    xn, xp, xo = (x + 1) % NX, (x + 3) % NX, (x + 2) % NX
+    near_extra, far_extra = yn == col, yp == col
+    order = [jnp.where(extra, a, b) for a, b in ((x, y), (xp, yp), (xn, yn), (xo, yo))]
 
     def is_me(pd, hdd):
         return jnp.logical_and(pd == p, hdd == hd)
@@ -104,52 +108,38 @@
     ready(yn * NZ + z, hd)
     ready(yp * NZ + z, hd)
     ready(p, sib)
-
-    @pl.when(extra)
-    def _():
-        for dz in range(NZ):
-            ready_unless_me(y * NZ + dz, z)
-        ready(yn * NZ + z, 2 * yn + c)
-        ready(yp * NZ + z, 2 * yp + c)
-
-    for slot in range(SLOTS):
-
-        @pl.when(pairs[slot] >= 0)
-        def _():
-            ready_unless_me(pairs[slot], home)
-
-    for h in range(HEADS):
-        pd, hdd, _ = owner_of(p, h, x, c)
-        ready_unless_me(pd, hdd)
-
-    @unless(last)
-    def _():
-        for h in range(HEADS):
-            pd, hdd, _ = owner_of(p + 1, h, x, c)
-            ready_unless_me(pd, hdd)
-        ready(p + 1, hd)
-
-    xn, xp, xo = (x + 1) % NX, (x + 3) % NX, (x + 2) % NX
     ready(p, 2 * xn + c)
     ready(p, 2 * xp + c)
 
+    @pl.when(extra)
+    def _():
+        for dz in range(NZ):
+            ready_unless_me(x * NZ + dz, home)
+
+    for slot in range(SLOTS):
+
+        @pl.when(pairs[slot] >= 0)
+        def _():
+            ready_unless_me(pairs[slot], home)
+
+    @unless(last)
+    def _():
+        ready(p + 1, hd)
+
     def count(flag):
         return flag.astype(jnp.int32)
 
     def others(pd, hdd):
         return 1 - count(is_me(pd, hdd))
 
-    expected = 2 + 1 + 2 + jnp.where(extra, 2, 0) + count(p > 0)
+    expected = 2 + 1 + 2 + count(p > 0)
     for k in range(2):
         for h in range(4):
             expected = expected + others(y * NZ + 4 * c + h, 2 * x + k)
-        expected = expected + others(y * NZ + hd, 2 * y + k)
+        expected = expected + others(x * NZ + x + 4 * c, 2 * y + k)
     for h in range(HEADS):
         pd, hdd, _ = owner_of(p, h, x, c)
         expected = expected + others(pd, hdd)
-    for slot in range(SLOTS):
-        for g in range(2):
-            expected = expected + jnp.where(pairs[slot] - 1 + g >= 0, others(pairs[slot] - 1 + g, home), 0)
 
     def put(src, dst, send, recv, pd, hdd):
         @pl.when(is_me(pd, hdd))
@@ -165,40 +155,58 @@
         def _():
             remote(src, dst, send, recv, pd, hdd).wait_send()
 
-    def kv_args(h, k):
-        src = k_in.at[:, pl.ds(h * HD, HD)] if k == 0 else vt.at[h]
+    def main_args(h, k):
+        src = k_in.at[:, pl.ds(pl.multiple_of(h * HD, HD), HD)] if k == 0 else vt.at[h]
         send = ksend.at[h] if k == 0 else vsend.at[h]
-        if h < 4:
-            return src, buf.at[jnp.where(y == x, 2, k), p], send, rmain.at[p], y * NZ + 4 * c + h, 2 * x + k
-        return src, buf.at[k, p], send, rextra.at[p], y * NZ + hd, 2 * y + k
+        return src, buf.at[jnp.where(y == h, 2, k), p], send, rmain.at[p], y * NZ + 4 * c + h, 2 * x + k
+
+    def extra_args(k):
+        src = k_in.at[:, pl.ds(4 * HD, HD)] if k == 0 else vt.at[4]
+        send = ksend.at[4] if k == 0 else vsend.at[4]
+        return src, buf.at[k, p], send, rextra.at[p], x * NZ + x + 4 * c, 2 * y + k
 
     def q_args(h):
         pd, hdd, slot = owner_of(p, h, x, c)
         return qt.at[h], qbuf.at[slot], qsend.at[h], qrecv.at[slot], pd, hdd
 
-    for i in range(3):
+    for i in range(2):
         loads[i].wait()
     for h in range(HEADS):
         for g in range(2):
             vt[h, g * TOK : (g + 1) * TOK, :] = v_in[g * TOK : (g + 1) * TOK, h * HD : (h + 1) * HD].T
+    for slot in range(3, SLOTS):
+
+        @pl.when(pairs[slot] < 0)
+        def _():
+            qbuf[slot] = jnp.zeros((HD, ROWS), bf16)
+
+    @pl.when(last)
+    def _():
+        att[TOK:, :] = jnp.zeros((TOK, WIDTH), bf16)
+
+    pl.semaphore_wait(barrier, expected)
+
+    def away(n):
+        return (z + jnp.where(n % 2 == 1, (n + 1) // 2, NZ - n // 2)) % NZ
+
+    def issue(n):
+        zd = away(n)
+
+        @pl.when(zd // 4 == c)
+        def _():
+            for k in range(2):
+                put(*main_args(zd % 4, k))
+
+        @pl.when(zd == x + 4 * c)
+        def _():
+            for k in range(2):
+                put(*extra_args(k))
+
+    for n in range(AHEAD):
+        issue(n)
+    loads[2].wait()
+    for h in range(HEADS):
         qt[h] = q_in[:, h * HD : (h + 1) * HD].T
-    for slot in range(3, SLOTS):
-
-        @pl.when(pairs[slot] < 0)
-        def _():
-            qbuf[slot] = jnp.zeros((HD, ROWS), bf16)
-
-    @pl.when(last)
-    def _():
-        att[TOK:, :] = jnp.zeros((TOK, WIDTH), bf16)
-
-    pl.semaphore_wait(barrier, expected)
-
-    for h in range(HEADS):
-        for k in range(2):
-            put(*kv_args(h, k))
-    for h in range(HEADS):
-        put(*q_args(h))
 
     for i in range(3, 6):
         loads[i].wait()
@@ -228,26 +236,39 @@
     def sibling(i):
         return remote(buf.at[c, i], buf.at[c, i], ssib.at[i], rsib.at[i], p, sib)
 
-    def ring(step, main):
+    def ring(main):
         if main:
             mine = jnp.where(extra, 2, c)
-            there_n, there_p = jnp.where(yn == x, 2, c), jnp.where(yp == x, 2, c)
-            hn, hp = hd, hd
+            there_n, there_p = jnp.where(near_extra, 2, c), jnp.where(far_extra, 2, c)
+            dev_n, dev_p = (yn * NZ + z, hd), (yp * NZ + z, hd)
+            here, after, before, opposite = y, yn, yp, yo
             sems, to_next, to_prev = rmain, snext, sprev
         else:
             mine, there_n, there_p = c, c, c
-            hn, hp = 2 * yn + c, 2 * yp + c
+            dev_n, dev_p = (p, 2 * xn + c), (p, 2 * xp + c)
+            here, after, before, opposite = x, xn, xp, xo
             sems, to_next, to_prev = rextra, enext, eprev
-        pn, pp = yn * NZ + z, yp * NZ + z
 
         def arrive(i):
-            remote(buf.at[mine, i], buf.at[mine, i], to_next.at[0], sems.at[i], pn, hn).wait_recv()
+            remote(buf.at[mine, i], buf.at[mine, i], to_next.at[0], sems.at[i], *dev_n).wait_recv()
 
         def go_next(i, s):
-            return remote(buf.at[mine, i], buf.at[there_n, i], to_next.at[s], sems.at[i], pn, hn)
+            return remote(buf.at[mine, i], buf.at[there_n, i], to_next.at[s], sems.at[i], *dev_n)
 
         def go_prev(i, s):
-            return remote(buf.at[mine, i], buf.at[there_p, i], to_prev.at[s], sems.at[i], pp, hp)
+            return remote(buf.at[mine, i], buf.at[there_p, i], to_prev.at[s], sems.at[i], *dev_p)
+
+        def when_next(even, act):
+            if main:
+                pl.when(jnp.logical_or(jnp.logical_not(near_extra), even))(act)
+            else:
+                act()
+
+        def when_prev(odd, act):
+            if main:
+                pl.when(jnp.logical_or(jnp.logical_not(far_extra), odd))(act)
+            else:
+                act()
 
         def across(i):
             if main:
@@ -258,59 +279,57 @@
             else:
                 sibling(i).start()
 
-        def own(b, carry):
-            i = y * NZ + b
+        def own(n):
+            i = here * NZ + away(n)
             arrive(i)
-            go_next(i, b).start()
-            go_prev(i, b).start()
+            when_next(n % 2 == 0, lambda: go_next(i, n).start())
+            when_prev(n % 2 == 1, lambda: go_prev(i, n).start())
             across(i)
-            return carry
-
-        def forward(b, carry):
-            i = yp * NZ + b
+
+        def forward(j):
+            i = before * NZ + away(2 * j)
             arrive(i)
-            go_next(i, 8 + b).start()
+            when_next(False, lambda: go_next(i, 8 + j).start())
             across(i)
-            i = yn * NZ + 4 + b
+            i = after * NZ + away(2 * j + 1)
             arrive(i)
-            go_prev(i, 8 + b).start()
+            when_prev(False, lambda: go_prev(i, 8 + j).start())
             across(i)
-            return carry
-
-        def rest(b, carry):
-            for i in (yp * NZ + 4 + b, yn * NZ + b):
+
+        def rest(j):
+            for i in (before * NZ + away(2 * j + 1), after * NZ + away(2 * j)):
                 arrive(i)
                 across(i)
-            return carry
-
-        def far_side(b, carry):
-            i = yo * NZ + b
+
+        def far_side(n):
+            i = opposite * NZ + away(n)
             arrive(i)
             across(i)
+
+        def close(n):
+            when_next(n % 2 == 0, lambda: go_next(n, n).wait_send())
+            when_prev(n % 2 == 1, lambda: go_prev(n, n).wait_send())
+
+        def close_forward(j):
+            when_next(False, lambda: go_next(j, 8 + j).wait_send())
+            when_prev(False, lambda: go_prev(j, 8 + j).wait_send())
+
+        return own, forward, rest, far_side, close, close_forward
+
+    main_ring, extra_ring = ring(True), ring(False)
+
+    def turns_of(step, length):
+        def one(n, carry):
+            if step == 0:
+                pl.when(n + AHEAD < NZ)(lambda: issue(n + AHEAD))
+            if step in (2, 3):
+                unless(extra)(lambda: main_ring[step](n))
+            else:
+                main_ring[step](n)
+            pl.when(extra)(lambda: extra_ring[step](n))
             return carry
 
-        def close(b, carry):
-            go_next(b, b).wait_send()
-            go_prev(b, b).wait_send()
-            return carry
-
-        if step == 0:
-            lax.fori_loop(0, NZ, own, 0)
-        elif step == 1:
-            lax.fori_loop(0, 4, forward, 0)
-        elif step == 2:
-            lax.fori_loop(0, 4, rest, 0)
-        elif step == 3:
-            lax.fori_loop(0, NZ, far_side, 0)
-        else:
-            lax.fori_loop(0, 12, close, 0)
-
-    def rings(step):
-        ring(step, True)
-
-        @pl.when(extra)
-        def _():
-            ring(step, False)
+        lax.fori_loop(0, length, one, 0)
 
     def from_sibling(quarter):
         def one(b, carry):
@@ -386,97 +405,138 @@
         def _():
             weigh(2 * turns - 1, p_b, keep_b)
 
-    rings(0)
-    rings(1)
-    from_sibling(y)
-    for slot in range(SLOTS):
-
-        @pl.when(pairs[slot] >= 0)
-        def _():
-            remote(qt.at[0], qbuf.at[slot], qsend.at[0], qrecv.at[slot], p, hd).wait_recv()
-
-    attend(y)
-    rings(2)
-    from_sibling(yp)
-    attend(yp)
-    from_sibling(yn)
-    attend(yn)
-    rings(3)
-    from_sibling(yo)
-    attend(yo)
+    pair_quarter = [pairs[slot] // NZ for slot in range(SLOTS)]
+
+    def stage_of(quarter):
+        stage = 0
+        for n in range(1, 4):
+            stage = jnp.where(order[n] == quarter, n, stage)
+        return stage
+
+    stages = [stage_of(quarter) for quarter in range(4)]
+    upto = [stages[0]]
+    for quarter in range(1, 4):
+        upto.append(jnp.maximum(upto[-1], stages[quarter]))
+
+    def pick_one(values, i):
+        chosen = values[0]
+        for n in range(1, len(values)):
+            chosen = jnp.where(i == n, values[n], chosen)
+        return chosen
 
     def o_args(slot, g):
-        pd = pairs[slot] - 1 + g
+        pd = pick_one(pairs, slot) - 1 + g
         dst = att.at[pl.ds((1 - g) * TOK, TOK), pl.ds(pl.multiple_of(head * HD, HD), HD)]
         return o_buf.at[slot, g], dst, osend.at[2 * slot + g], orecv.at[(1 - g) * HEADS + head], pd, home
 
+    def finish(stage):
+        def one(slot, carry):
+            pair = pick_one(pairs, slot)
+
+            @pl.when(jnp.logical_and(pair >= 0, pick_one(upto, pair // NZ) == stage))
+            def _():
+                mixed = acc[slot, :HD] / acc[slot, HD : HD + 1]
+                o_buf[slot, 1] = mixed[:, TOK:].T.astype(bf16)
+                put(*o_args(slot, 1))
+                o_buf[slot, 0] = mixed[:, :TOK].T.astype(bf16)
+
+                @pl.when(pair >= 1)
+                def _():
+                    put(*o_args(slot, 0))
+
+            return carry
+
+        lax.fori_loop(0, SLOTS, one, 0)
+
+    turns_of(0, NZ)
+    for h in range(HEADS):
+        put(*q_args(h))
+    turns_of(1, 4)
+    from_sibling(order[0])
     for slot in range(SLOTS):
 
         @pl.when(pairs[slot] >= 0)
         def _():
-            mixed = acc[slot, :HD] / acc[slot, HD : HD + 1]
-            for g in range(2):
-                o_buf[slot, g] = mixed[:, g * TOK : (g + 1) * TOK].T.astype(bf16)
-            put(*o_args(slot, 1))
-
-        @pl.when(pairs[slot] >= 1)
-        def _():
-            put(*o_args(slot, 0))
+            remote(qt.at[0], qbuf.at[slot], qsend.at[0], qrecv.at[slot], p, hd).wait_recv()
+
+    attend(order[0])
+    finish(0)
+    turns_of(2, 4)
+    from_sibling(order[1])
+    attend(order[1])
+    finish(1)
+    from_sibling(order[2])
+    attend(order[2])
+    finish(2)
+    turns_of(3, NZ)
+    from_sibling(order[3])
+    attend(order[3])
+    finish(3)
 
     def o_arrive(g):
         for h in range(HEADS):
             dst = att.at[pl.ds(g * TOK, TOK), pl.ds(h * HD, HD)]
             remote(dst, dst, osend.at[0], orecv.at[g * HEADS + h], p, hd).wait_recv()
 
-    o_arrive(0)
-
-    @unless(last)
-    def _():
-        o_arrive(1)
+    turn = (xo, xn, xp, x)
+
+    def half_rows(t):
+        return slice(t * TOK, (t + 1) * TOK)
+
+    def part(t, j, core):
+        cols = pl.ds(pl.multiple_of((2 * turn[j] + core) * WIDTH, HD), WIDTH)
+        return jnp.dot(att[half_rows(t), :], w[:, cols], preferred_element_type=f32)
+
+    def over(t, j):
+        return remote(s1.at[t, j], r1.at[t, j], send1.at[4 * t + j], recv1.at[4 * t + j], p, sib)
+
+    def far_copy(t):
+        return remote(far.at[t], far_in.at[t], fsend.at[t], frecv.at[t], p, 2 * (xn, xp)[t] + c)
+
+    def near_copy(t, d):
+        i = 2 * t + d
+        return remote(near.at[t, d], near_in.at[t, d], nsend.at[i], nrecv.at[i], p, 2 * (xn, xp)[d] + c)
+
+    def send_parts(t):
+        for j in range(4):
+            s1[t, j] = part(t, j, 1 - c).astype(bf16)
+            over(t, j).start()
+
+        def both(j):
+            mine = part(t, j, c)
+            over(t, j).wait_recv()
+            return mine + r1[t, j].astype(f32)
+
+        far[t] = both(0).astype(bf16)
+        far_copy(t).start()
+        through, direct = t, 1 - t
+        near[t, direct] = both(1 + direct).astype(bf16)
+        near_copy(t, direct).start()
+        through_sum = both(1 + through)
+        keep[half_rows(t), :] = both(3)
+        far_copy(t).wait_recv()
+        near[t, through] = (through_sum + far_in[t].astype(f32)).astype(bf16)
+        near_copy(t, through).start()
+
+    def all_parts(t):
+        total = keep[half_rows(t), :]
+        for d in (1 - t, t):
+            near_copy(t, d).wait_recv()
+            total = total + near_in[t, d].astype(f32)
+        return total
 
     loads[6].wait()
     loads[7].wait()
-
-    def part(xd, core):
-        cols = pl.ds(pl.multiple_of((2 * xd + core) * WIDTH, HD), WIDTH)
-        return jnp.dot(att[...], w[:, cols], preferred_element_type=f32)
-
-    turn = (xo, xn, xp, x)
-
-    def over(j):
-        return remote(s1.at[j], r1.at[j], send1.at[j], recv1.at[j], p, sib)
-
-    def far_copy(d):
-        return remote(far.at[pl.ds(d * TOK, TOK)], far_in.at[d], fsend.at[d], frecv.at[d], p, 2 * (xn, xp)[d] + c)
-
-    def near_copy(d):
-        return remote(near.at[d], near_in.at[d], nsend.at[d], nrecv.at[d], p, 2 * (xn, xp)[d] + c)
-
-    for j in range(4):
-        s1[j] = part(turn[j], 1 - c).astype(bf16)
-        over(j).start()
-
-    def both(j):
-        mine = part(turn[j], c)
-        over(j).wait_recv()
-        return mine + r1[j].astype(f32)
-
-    far[...] = both(0).astype(bf16)
-    far_copy(0).start()
-    far_copy(1).start()
-    for d in range(2):
-        mine = both(1 + d)
-        far_copy(d).wait_recv()
-        near[d, (1 - d) * TOK : (2 - d) * TOK] = mine[(1 - d) * TOK : (2 - d) * TOK].astype(bf16)
-        rows = slice(d * TOK, (d + 1) * TOK)
-        near[d, rows] = (mine[rows] + far_in[d].astype(f32)).astype(bf16)
-        near_copy(d).start()
-    summed = both(3)
-    for d in range(2):
-        near_copy(d).wait_recv()
-        summed = summed + near_in[d].astype(f32)
-
-    out_ref[:TOK, :] = (hid[TOK:, :].astype(f32) + gate[pl.ds(levels[1], 1), :] * summed[:TOK]).astype(bf16)
+    o_arrive(0)
+    send_parts(0)
+
+    @unless(last)
+    def _():
+        o_arrive(1)
+
+    send_parts(1)
+    out_ref[:TOK, :] = (hid[TOK:, :].astype(f32) + gate[pl.ds(levels[1], 1), :] * all_parts(0)).astype(bf16)
+    summed = all_parts(1)
 
     @pl.when(last)
     def _():
@@ -486,7 +546,7 @@
     def _():
         for copy in shift:
             copy.wait_recv()
-        out_ref[TOK:, :] = (hs[...].astype(f32) + gs[0:1, :] * summed[TOK:]).astype(bf16)
+        out_ref[TOK:, :] = (hs[...].astype(f32) + gs[0:1, :] * summed).astype(bf16)
 
     @pl.when(p > 0)
     def _():
@@ -495,9 +555,10 @@
 
     for h in range(HEADS):
         for k in range(2):
-            put_done(*kv_args(h, k))
+            put_done(*(main_args(h, k) if h < 4 else extra_args(k)))
         put_done(*q_args(h))
-    rings(4)
+    turns_of(4, NZ)
+    turns_of(5, 4)
 
     def sibling_done(i, carry):
         sibling(i).wait_send()
@@ -514,11 +575,12 @@
         def _():
             put_done(*o_args(slot, 0))
 
-    for j in range(4):
-        over(j).wait_send()
-    for d in range(2):
-        far_copy(d).wait_send()
-        near_copy(d).wait_send()
+    for t in range(2):
+        for j in range(4):
+            over(t, j).wait_send()
+        far_copy(t).wait_send()
+        for d in range(2):
+            near_copy(t, d).wait_send()
 
 
 def on_device(query_states, key_states, value_states, hidden, out_weight, gate_table, levels, visible, incoming):
@@ -553,12 +615,13 @@
             vmem((SLOTS, HD + 16, ROWS), f32),
             vmem((SLOTS, 2, TOK, HD), bf16),
             vmem((ROWS, WIDTH), bf16),
-            vmem((4, ROWS, WIDTH), bf16),
-            vmem((4, ROWS, WIDTH), bf16),
-            vmem((ROWS, WIDTH), bf16),
+            vmem((2, 4, TOK, WIDTH), bf16),
+            vmem((2, 4, TOK, WIDTH), bf16),
             vmem((2, TOK, WIDTH), bf16),
-            vmem((2, ROWS, WIDTH), bf16),
-            vmem((2, ROWS, WIDTH), bf16),
+            vmem((2, TOK, WIDTH), bf16),
+            vmem((2, 2, TOK, WIDTH), bf16),
+            vmem((2, 2, TOK, WIDTH), bf16),
+            vmem((ROWS, WIDTH), f32),
             vmem((TOK, WIDTH), bf16),
             vmem((8, WIDTH), f32),
             vmem((8, WIDTH), f32),
@@ -577,12 +640,12 @@
             dma((PAIRS,)),
             dma((2 * SLOTS,)),
             dma((2 * HEADS,)),
+            dma((8,)),
+            dma((8,)),
+            dma((2,)),
+            dma((2,)),
             dma((4,)),
             dma((4,)),
-            dma((2,)),
-            dma((2,)),
-            dma((2,)),
-            dma((2,)),
             dma((2,)),
             dma((2,)),
         ],

time: 113 us -> 96.1 us (0.85)
  the two profiles are of different devices: /device:TPU:102 before, /device:TPU:1 now
where the time goes in v3:
time: 96.1 us; the launch traced here: 94.4 us
  Pallas kernels  92.7 us (96%)
  local copies, waits for them, and re-layouts  1.73 us (2%)
    pallas_call x1, Pallas kernels, on_device(): pl.pallas_call(body, out_shape=jax.ShapeDtypeStruct((ROWS, WIDTH), bf16),...  92.7 us

profile of v3, /device:TPU:1, one launch (start us, length us, event | category | flops | bytes accessed | tf_op | source)
XLA Modules:
  0.0 94.4 jit_solution(8312470779331518009)
XLA Ops:
  0.0 92.7 %block.1 = bf16[256,640]{1,0:T(8,128)(2,1)} custom-call(bf16[256,640]{1,0:T(8,128)(2,1)} %q_hbm.1, bf16[256,640]{1,0:T(8,128)(2,1)} %k_hbm.1, bf16[256,640]{1,0:T(8,128)(2,1)} %v_hbm.1, bf16[256,640]{1,0:T(8,128)(2,1)} %hid_hbm.1, bf16[640,5120]{1,0:T(8,128)(2,1)} %w_hbm.1, f32[1000,640]{1,0:T(8,128)} %gate_hbm.1, s32[2]{0:T(128)} %levels.1, ...), custom_call_target="tpu_custom_call" | custom-call | tf_op jit(solution)/shard_map/block/pallas_call | solution.py:589
  92.7 1.7 %copy.11 = bf16[256,640]{1,0:T(8,128)(2,1)} copy(bf16[256,640]{1,0:T(8,128)(2,1)} %block.1) | data formatting | bytes 655360

commit v4 on v3

--- a/solution.py
+++ b/solution.py
@@ -21,7 +21,8 @@
 KEYS = CHUNK * ROWS
 PARTS = 2 * CHUNK
 PER_QUARTER = NZ // CHUNK
-AHEAD = 4
+AHEAD = 8
+QUERIES_AT = 4
 MASKED = -1e30
 LOWEST = -1e20
 MESH = pl.DeviceIdType.MESH
@@ -318,9 +319,14 @@
 
     main_ring, extra_ring = ring(True), ring(False)
 
+    def send_queries():
+        for h in range(HEADS):
+            put(*q_args(h))
+
     def turns_of(step, length):
         def one(n, carry):
             if step == 0:
+                pl.when(n == QUERIES_AT)(send_queries)
                 pl.when(n + AHEAD < NZ)(lambda: issue(n + AHEAD))
             if step in (2, 3):
                 unless(extra)(lambda: main_ring[step](n))
@@ -429,28 +435,24 @@
         dst = att.at[pl.ds((1 - g) * TOK, TOK), pl.ds(pl.multiple_of(head * HD, HD), HD)]
         return o_buf.at[slot, g], dst, osend.at[2 * slot + g], orecv.at[(1 - g) * HEADS + head], pd, home
 
+    def mix(slot, g):
+        cols = slice(g * TOK, (g + 1) * TOK)
+        o_buf[slot, g] = (acc[slot, :HD, cols] / acc[slot, HD : HD + 1, cols]).T.astype(bf16)
+
     def finish(stage):
         def one(slot, carry):
             pair = pick_one(pairs, slot)
 
             @pl.when(jnp.logical_and(pair >= 0, pick_one(upto, pair // NZ) == stage))
             def _():
-                mixed = acc[slot, :HD] / acc[slot, HD : HD + 1]
-                o_buf[slot, 1] = mixed[:, TOK:].T.astype(bf16)
+                mix(slot, 1)
                 put(*o_args(slot, 1))
-                o_buf[slot, 0] = mixed[:, :TOK].T.astype(bf16)
-
-                @pl.when(pair >= 1)
-                def _():
-                    put(*o_args(slot, 0))
 
             return carry
 
         lax.fori_loop(0, SLOTS, one, 0)
 
     turns_of(0, NZ)
-    for h in range(HEADS):
-        put(*q_args(h))
     turns_of(1, 4)
     from_sibling(order[0])
     for slot in range(SLOTS):
@@ -466,12 +468,26 @@
     attend(order[1])
     finish(1)
     from_sibling(order[2])
+    turns_of(3, NZ)
     attend(order[2])
     finish(2)
-    turns_of(3, NZ)
     from_sibling(order[3])
     attend(order[3])
     finish(3)
+
+    def second_half(slot, carry):
+        @pl.when(pick_one(pairs, slot) >= 0)
+        def _():
+            mix(slot, 0)
+            put_done(*o_args(slot, 1))
+
+        @pl.when(pick_one(pairs, slot) >= 1)
+        def _():
+            put(*o_args(slot, 0))
+
+        return carry
+
+    lax.fori_loop(0, SLOTS, second_half, 0)
 
     def o_arrive(g):
         for h in range(HEADS):
@@ -498,22 +514,26 @@
         return remote(near.at[t, d], near_in.at[t, d], nsend.at[i], nrecv.at[i], p, 2 * (xn, xp)[d] + c)
 
     def send_parts(t):
-        for j in range(4):
+        through, direct = t, 1 - t
+
+        def for_sibling(j):
             s1[t, j] = part(t, j, 1 - c).astype(bf16)
             over(t, j).start()
 
-        def both(j):
-            mine = part(t, j, c)
+        def both(j, mine):
             over(t, j).wait_recv()
             return mine + r1[t, j].astype(f32)
 
-        far[t] = both(0).astype(bf16)
+        for_sibling(0)
+        for_sibling(1 + direct)
+        far[t] = both(0, part(t, 0, c)).astype(bf16)
         far_copy(t).start()
-        through, direct = t, 1 - t
-        near[t, direct] = both(1 + direct).astype(bf16)
+        near[t, direct] = both(1 + direct, part(t, 1 + direct, c)).astype(bf16)
         near_copy(t, direct).start()
-        through_sum = both(1 + through)
-        keep[half_rows(t), :] = both(3)
+        for_sibling(1 + through)
+        for_sibling(3)
+        through_sum = both(1 + through, part(t, 1 + through, c))
+        keep[half_rows(t), :] = both(3, part(t, 3, c))
         far_copy(t).wait_recv()
         near[t, through] = (through_sum + far_in[t].astype(f32)).astype(bf16)
         near_copy(t, through).start()
@@ -566,10 +586,6 @@
 
     lax.fori_loop(0, PAIRS, sibling_done, 0)
     for slot in range(SLOTS):
-
-        @pl.when(pairs[slot] >= 0)
-        def _():
-            put_done(*o_args(slot, 1))
 
         @pl.when(pairs[slot] >= 1)
         def _():

time: 96.1 us -> 90.2 us (0.939)
  Pallas kernels: 92.7 us -> 87.7 us
    pallas_call x1, Pallas kernels: 92.7 us -> 87.7 us  [on_device(): pl.pallas_call(body, out_shape=jax.ShapeDtypeStruct((ROWS, WIDTH), bf16),...]
where the time goes in v4:
time: 90.2 us; the launch traced here: 89.5 us
  Pallas kernels  87.7 us (97%)
  local copies, waits for them, and re-layouts  1.73 us (2%)
    pallas_call x1, Pallas kernels, on_device(): pl.pallas_call(body, out_shape=jax.ShapeDtypeStruct((ROWS, WIDTH), bf16),...  87.7 us

profile of v4, /device:TPU:1, one launch (start us, length us, event | category | flops | bytes accessed | tf_op | source)
XLA Modules:
  0.0 89.5 jit_solution(5020512384981737538)
XLA Ops:
  0.0 87.7 %block.1 = bf16[256,640]{1,0:T(8,128)(2,1)} custom-call(bf16[256,640]{1,0:T(8,128)(2,1)} %q_hbm.1, bf16[256,640]{1,0:T(8,128)(2,1)} %k_hbm.1, bf16[256,640]{1,0:T(8,128)(2,1)} %v_hbm.1, bf16[256,640]{1,0:T(8,128)(2,1)} %hid_hbm.1, bf16[640,5120]{1,0:T(8,128)(2,1)} %w_hbm.1, f32[1000,640]{1,0:T(8,128)} %gate_hbm.1, s32[2]{0:T(128)} %levels.1, ...), custom_call_target="tpu_custom_call" | custom-call | tf_op jit(solution)/shard_map/block/pallas_call | solution.py:605
  87.7 1.7 %copy.11 = bf16[256,640]{1,0:T(8,128)(2,1)} copy(bf16[256,640]{1,0:T(8,128)(2,1)} %block.1) | data formatting | bytes 655360

commit v5 on v4

--- a/solution.py
+++ b/solution.py
@@ -23,6 +23,7 @@
 PER_QUARTER = NZ // CHUNK
 AHEAD = 8
 QUERIES_AT = 4
+PIECES = 4
 MASKED = -1e30
 LOWEST = -1e20
 MESH = pl.DeviceIdType.MESH
@@ -506,12 +507,20 @@
     def over(t, j):
         return remote(s1.at[t, j], r1.at[t, j], send1.at[4 * t + j], recv1.at[4 * t + j], p, sib)
 
-    def far_copy(t):
-        return remote(far.at[t], far_in.at[t], fsend.at[t], frecv.at[t], p, 2 * (xn, xp)[t] + c)
-
-    def near_copy(t, d):
-        i = 2 * t + d
-        return remote(near.at[t, d], near_in.at[t, d], nsend.at[i], nrecv.at[i], p, 2 * (xn, xp)[d] + c)
+    piece = TOK // PIECES
+
+    def piece_rows(u):
+        return slice(u * piece, (u + 1) * piece)
+
+    def far_copy(t, u):
+        i = PIECES * t + u
+        rows = pl.ds(u * piece, piece)
+        return remote(far.at[t, rows], far_in.at[t, rows], fsend.at[i], frecv.at[i], p, 2 * (xn, xp)[t] + c)
+
+    def near_copy(t, d, u):
+        i = PIECES * (2 * t + d) + u
+        rows = pl.ds(u * piece, piece)
+        return remote(near.at[t, d, rows], near_in.at[t, d, rows], nsend.at[i], nrecv.at[i], p, 2 * (xn, xp)[d] + c)
 
     def send_parts(t):
         through, direct = t, 1 - t
@@ -527,21 +536,26 @@
         for_sibling(0)
         for_sibling(1 + direct)
         far[t] = both(0, part(t, 0, c)).astype(bf16)
-        far_copy(t).start()
+        for u in range(PIECES):
+            far_copy(t, u).start()
         near[t, direct] = both(1 + direct, part(t, 1 + direct, c)).astype(bf16)
-        near_copy(t, direct).start()
+        for u in range(PIECES):
+            near_copy(t, direct, u).start()
         for_sibling(1 + through)
         for_sibling(3)
         through_sum = both(1 + through, part(t, 1 + through, c))
         keep[half_rows(t), :] = both(3, part(t, 3, c))
-        far_copy(t).wait_recv()
-        near[t, through] = (through_sum + far_in[t].astype(f32)).astype(bf16)
-        near_copy(t, through).start()
+        for u in range(PIECES):
+            rows = piece_rows(u)
+            far_copy(t, u).wait_recv()
+            near[t, through, rows] = (through_sum[rows] + far_in[t, rows].astype(f32)).astype(bf16)
+            near_copy(t, through, u).start()
 
     def all_parts(t):
         total = keep[half_rows(t), :]
         for d in (1 - t, t):
-            near_copy(t, d).wait_recv()
+            for u in range(PIECES):
+                near_copy(t, d, u).wait_recv()
             total = total + near_in[t, d].astype(f32)
         return total
 
@@ -594,9 +608,10 @@
     for t in range(2):
         for j in range(4):
             over(t, j).wait_send()
-        far_copy(t).wait_send()
-        for d in range(2):
-            near_copy(t, d).wait_send()
+        for u in range(PIECES):
+            far_copy(t, u).wait_send()
+            for d in range(2):
+                near_copy(t, d, u).wait_send()
 
 
 def on_device(query_states, key_states, value_states, hidden, out_weight, gate_table, levels, visible, incoming):
@@ -658,10 +673,10 @@
             dma((2 * HEADS,)),
             dma((8,)),
             dma((8,)),
-            dma((2,)),
-            dma((2,)),
-            dma((4,)),
-            dma((4,)),
+            dma((2 * PIECES,)),
+            dma((2 * PIECES,)),
+            dma((4 * PIECES,)),
+            dma((4 * PIECES,)),
             dma((2,)),
             dma((2,)),
         ],

time: 90.2 us -> 88.3 us (0.979)
  Pallas kernels: 87.7 us -> 85.9 us
    pallas_call x1, Pallas kernels: 87.7 us -> 85.9 us  [on_device(): pl.pallas_call(body, out_shape=jax.ShapeDtypeStruct((ROWS, WIDTH), bf16),...]
where the time goes in v5:
time: 88.3 us; the launch traced here: 87.6 us
  Pallas kernels  85.9 us (97%)
  local copies, waits for them, and re-layouts  1.73 us (2%)
    pallas_call x1, Pallas kernels, on_device(): pl.pallas_call(body, out_shape=jax.ShapeDtypeStruct((ROWS, WIDTH), bf16),...  85.9 us

profile of v5, /device:TPU:1, one launch (start us, length us, event | category | flops | bytes accessed | tf_op | source)
XLA Modules:
  0.0 87.6 jit_solution(13670084106176044691)
XLA Ops:
  0.0 85.9 %block.1 = bf16[256,640]{1,0:T(8,128)(2,1)} custom-call(bf16[256,640]{1,0:T(8,128)(2,1)} %q_hbm.1, bf16[256,640]{1,0:T(8,128)(2,1)} %k_hbm.1, bf16[256,640]{1,0:T(8,128)(2,1)} %v_hbm.1, bf16[256,640]{1,0:T(8,128)(2,1)} %hid_hbm.1, bf16[640,5120]{1,0:T(8,128)(2,1)} %w_hbm.1, f32[1000,640]{1,0:T(8,128)} %gate_hbm.1, s32[2]{0:T(128)} %levels.1, ...), custom_call_target="tpu_custom_call" | custom-call | tf_op jit(solution)/shard_map/block/pallas_call | solution.py:620
  85.9 1.7 %copy.11 = bf16[256,640]{1,0:T(8,128)(2,1)} copy(bf16[256,640]{1,0:T(8,128)(2,1)} %block.1) | data formatting | bytes 655360

commit v6 on v5

--- a/solution.py
+++ b/solution.py
@@ -544,12 +544,12 @@
         for_sibling(1 + through)
         for_sibling(3)
         through_sum = both(1 + through, part(t, 1 + through, c))
-        keep[half_rows(t), :] = both(3, part(t, 3, c))
         for u in range(PIECES):
             rows = piece_rows(u)
             far_copy(t, u).wait_recv()
             near[t, through, rows] = (through_sum[rows] + far_in[t, rows].astype(f32)).astype(bf16)
             near_copy(t, through, u).start()
+        keep[half_rows(t), :] = both(3, part(t, 3, c))
 
     def all_parts(t):
         total = keep[half_rows(t), :]

time: 88.3 us -> 89 us (level)
  no operation moved by 1% of the time
where the time goes in v6:
time: 89 us; the launch traced here: 88.3 us
  Pallas kernels  86.6 us (97%)
  local copies, waits for them, and re-layouts  1.73 us (2%)
    pallas_call x1, Pallas kernels, on_device(): pl.pallas_call(body, out_shape=jax.ShapeDtypeStruct((ROWS, WIDTH), bf16),...  86.6 us

profile of v6, /device:TPU:1, one launch (start us, length us, event | category | flops | bytes accessed | tf_op | source)
XLA Modules:
  0.0 88.3 jit_solution(1797665939293864187)
XLA Ops:
  0.0 86.6 %block.1 = bf16[256,640]{1,0:T(8,128)(2,1)} custom-call(bf16[256,640]{1,0:T(8,128)(2,1)} %q_hbm.1, bf16[256,640]{1,0:T(8,128)(2,1)} %k_hbm.1, bf16[256,640]{1,0:T(8,128)(2,1)} %v_hbm.1, bf16[256,640]{1,0:T(8,128)(2,1)} %hid_hbm.1, bf16[640,5120]{1,0:T(8,128)(2,1)} %w_hbm.1, f32[1000,640]{1,0:T(8,128)} %gate_hbm.1, s32[2]{0:T(128)} %levels.1, ...), custom_call_target="tpu_custom_call" | custom-call | tf_op jit(solution)/shard_map/block/pallas_call | solution.py:620
  86.6 1.7 %copy.11 = bf16[256,640]{1,0:T(8,128)(2,1)} copy(bf16[256,640]{1,0:T(8,128)(2,1)} %block.1) | data formatting | bytes 655360
